TPU v7x, 512 devices: a whole 4x4x16 slice. The times are simulated.
512 devices in a mesh: seq: 32 (over x, y, core), expert: 16 (over z).
Axes of the slice: x: 4, y: 4, z: 16, core: 2. Of those that a mesh axis runs over, the one named last changes fastest.
Arguments:
- tokens: bfloat16 [1, 32768, 2048], P(None, 'seq', 'expert'), may hold values from -6 to 6
- slot_params: bfloat16 [256, 2048], P('expert'), may hold values from -16 to 16
- w_in: bfloat16 [16, 2048, 4096], P('expert', None, 'seq'), may hold values from -0.125 to 0.125
- w_out: bfloat16 [16, 4096, 2048], P('expert', 'seq'), may hold values from -0.09375 to 0.09375
- out_grad: bfloat16 [1, 32768, 2048], P(None, 'seq', 'expert'), may hold values from -6 to 6
Outputs:
- mixed: bfloat16 [1, 32768, 2048], P(None, 'seq', 'expert')
- token_grad: bfloat16 [1, 32768, 2048], P(None, 'seq', 'expert')
- param_grad: bfloat16 [256, 2048], P('expert')
- w_in_grad: bfloat16 [16, 2048, 4096], P('expert', None, 'seq')
- w_out_grad: bfloat16 [16, 4096, 2048], P('expert', 'seq')
All inputs are finite; a program needn't handle non-finite values.
Results may differ from a plain program's by a relative error of at most 0.033.
Values may be sent and summed in bfloat16 or wider, within the bound.
No kernel may reach another device: no remote copies, remote signals or barrier semaphores. Data moves between devices by JAX's collectives and lax.ppermute only.
A program may use at most 64 MiB of HBM per device.

v0:
```python
import jax
import jax.numpy as jnp
from jax import lax
from jax.sharding import PartitionSpec as P


def gelu_exact(values):
    return jax.nn.gelu(values, approximate=False)


def soft_dispatch(logits, values):
    maximum = lax.pmax(jnp.max(logits, axis=2), "seq")
    raised = jnp.exp(logits - maximum[:, :, None])
    denominator = lax.psum(jnp.sum(raised, axis=2), "seq")
    dispatch = raised / denominator[:, :, None]
    dispatch_low = dispatch.astype(jnp.bfloat16)
    slot_partial = jnp.einsum(
        "sct,ctd->scd", dispatch_low, values, preferred_element_type=jnp.float32
    )
    slot_in = lax.psum(slot_partial, "seq")
    return (dispatch, dispatch_low, slot_in)


def expert_forward(slot_low, w_in, w_out):
    width = slot_low.shape[2]
    slot_rows = slot_low.reshape(-1, width)
    preact = jnp.dot(slot_rows, w_in[0], preferred_element_type=jnp.float32)
    hidden_low = gelu_exact(preact).astype(jnp.bfloat16)
    expert_part = jnp.dot(hidden_low, w_out[0], preferred_element_type=jnp.float32)
    expert_out = lax.psum(expert_part, "seq")
    out_low = expert_out.astype(jnp.bfloat16).reshape(slot_low.shape)
    out_slices = lax.all_to_all(out_low, "expert", split_axis=2, concat_axis=0, tiled=True)
    return (slot_rows, preact, hidden_low, out_low, out_slices)


def soft_combine(all_logits, out_slices):
    combine_peak = jnp.max(all_logits, axis=0)
    lifted = jnp.exp(all_logits - combine_peak[None])
    combine = lifted / jnp.sum(lifted, axis=0)[None]
    combine_low = combine.astype(jnp.bfloat16)
    mixed = jnp.einsum(
        "nct,ncd->ctd", combine_low, out_slices, preferred_element_type=jnp.float32
    ).astype(jnp.bfloat16)
    return (combine, combine_low, mixed)


def expert_backward(slot_grad_low, slot_rows, preact, hidden_low, w_in, w_out):
    width = slot_grad_low.shape[2]
    grad_rows = slot_grad_low.reshape(-1, width)
    w_out_grad = jnp.dot(hidden_low.T, grad_rows, preferred_element_type=jnp.float32).astype(
        jnp.bfloat16
    )
    hidden_grad = jnp.dot(grad_rows, w_out[0].T, preferred_element_type=jnp.float32)
    unused, pullback = jax.vjp(gelu_exact, preact)
    preact_low = pullback(hidden_grad)[0].astype(jnp.bfloat16)
    w_in_grad = jnp.dot(slot_rows.T, preact_low, preferred_element_type=jnp.float32).astype(
        jnp.bfloat16
    )
    input_part = jnp.dot(preact_low, w_in[0].T, preferred_element_type=jnp.float32)
    input_grad = lax.psum(input_part.astype(jnp.bfloat16), "seq")
    input_low = input_grad.reshape(slot_grad_low.shape)
    return (input_low, w_in_grad, w_out_grad)


def local(tokens, slot_params, w_in, w_out, out_grad):
    bfloat = jnp.bfloat16
    single = jnp.float32
    slots = slot_params.shape[0]
    own_first = lax.axis_index("expert") * slots
    features = lax.all_gather(tokens, "expert", axis=2, tiled=True)
    param_rows = lax.all_gather(slot_params, "expert", axis=0, tiled=True)
    all_logits = jnp.einsum("nd,ctd->nct", param_rows, features, preferred_element_type=single)
    logits = lax.dynamic_slice_in_dim(all_logits, own_first, slots, 0)
    dispatch, dispatch_low, slot_in = soft_dispatch(logits, features)
    slot_low = slot_in.astype(bfloat)
    slot_rows, preact, hidden_low, out_low, out_slices = expert_forward(slot_low, w_in, w_out)
    combine, combine_low, mixed = soft_combine(all_logits, out_slices)
    combine_own = lax.dynamic_slice_in_dim(combine, own_first, slots, 0)
    combine_own_low = lax.dynamic_slice_in_dim(combine_low, own_first, slots, 0)
    grad_features = lax.all_gather(out_grad, "expert", axis=2, tiled=True)
    combine_cot = jnp.einsum("scd,ctd->sct", out_low, grad_features, preferred_element_type=single)
    slot_grad_part = jnp.einsum(
        "sct,ctd->scd", combine_own_low, grad_features, preferred_element_type=single
    )
    slot_grad = lax.psum(slot_grad_part, "seq")
    slot_grad_low = slot_grad.astype(bfloat)
    row_part = jnp.sum(combine_own_low.astype(single) * combine_cot, axis=0)
    row_sum = lax.psum(row_part, "expert")
    combine_term = combine_own * (combine_cot - row_sum[None])
    input_low, w_in_grad, w_out_grad = expert_backward(
        slot_grad_low, slot_rows, preact, hidden_low, w_in, w_out
    )
    dispatch_cot = jnp.einsum("scd,ctd->sct", input_low, features, preferred_element_type=single)
    column_part = jnp.sum(dispatch_low.astype(single) * dispatch_cot, axis=2)
    column_sum = lax.psum(column_part, "seq")
    logit_low = (dispatch * (dispatch_cot - column_sum[:, :, None]) + combine_term).astype(bfloat)
    param_part = jnp.einsum("sct,ctd->sd", logit_low, features, preferred_element_type=single)
    param_grad = lax.psum(param_part, "seq").astype(bfloat)
    weights_all, logit_all = (
        lax.all_gather(dispatch_low, "expert", axis=0, tiled=True),
        lax.all_gather(logit_low, "expert", axis=0, tiled=True),
    )
    input_slices = lax.all_to_all(input_low, "expert", split_axis=2, concat_axis=0, tiled=True)
    slice_width = input_slices.shape[2]
    param_slices = lax.dynamic_slice_in_dim(
        param_rows, lax.axis_index("expert") * slice_width, slice_width, 1
    )
    token_part = jnp.einsum(
        "nct,ncd->ctd", weights_all, input_slices, preferred_element_type=single
    )
    token_part = token_part + jnp.einsum(
        "nct,nd->ctd", logit_all, param_slices, preferred_element_type=single
    )
    token_grad = token_part.astype(bfloat)
    return (mixed, token_grad, param_grad, w_in_grad[None], w_out_grad[None])


def solution(mesh):
    return jax.shard_map(
        local,
        mesh=mesh,
        in_specs=(
            P(None, "seq", "expert"),
            P("expert", None),
            P("expert", None, "seq"),
            P("expert", "seq", None),
            P(None, "seq", "expert"),
        ),
        out_specs=(
            P(None, "seq", "expert"),
            P(None, "seq", "expert"),
            P("expert", None),
            P("expert", None, "seq"),
            P("expert", "seq", None),
        ),
        check_vma=False,
    )
```

profile of v0, /device:TPU:64, one launch (start us, length us, event | category | flops | bytes accessed | tf_op | source)
XLA Modules:
  0.0 981.1 jit_solution(9180862646416644525)
XLA Ops:
  9.5 74.4 %all-gather.5.cloned.1.call-done = bf16[256,2048]{1,0:T(8,128)(2,1)} async-done(((bf16[16,2048]{1,0:T(8,128)(2,1)}), bf16[256,2048]{1,0:T(8,128)(2,1)}) %all-gather.5.cloned.1.call-update) | async-done | bytes 1048592 | tf_op jit(solution)/shard_map/all_gather | solution.py:71
  83.8 94.1 %all-gather.7.cloned.1.call-done = bf16[1,1024,2048]{2,1,0:T(8,128)(2,1)} async-done(((bf16[1,1024,128]{2,1,0:T(8,128)(2,1)}), bf16[1,1024,2048]{2,1,0:T(8,128)(2,1)}) %all-gather.7.cloned.1.call-update) | async-done | bytes 4194320 | tf_op jit(solution)/shard_map/all_gather | solution.py:70
  178.0 3.8 fusion.72
  181.9 62.7 %pmax.7 = f32[16]{0:T(128)S(1)} all-reduce(f32[16]{0:T(128)S(1)} %dynamic-slice_reduce_fusion), channel_id=1, replica_groups=mesh['seq'=32,'expert'=16] {'seq'}, use_global_device_ids=true, to_apply=%region_3.0 | all-reduce | flops 16 | bytes 128 | tf_op jit(solution)/shard_map/pmax | solution.py:12
  244.8 62.7 %psum.56 = f32[16]{0:T(128)S(1)} all-reduce(f32[16]{0:T(128)S(1)} %fusion.49), channel_id=1, replica_groups=mesh['seq'=32,'expert'=16] {'seq'}, use_global_device_ids=true, to_apply=%region_5.0 | all-reduce | flops 16 | bytes 128 | tf_op jit(solution)/shard_map/psum | solution.py:14
  307.5 2.8 fusion.14
  310.6 32.3 %all-gather = bf16[256,1024]{1,0:T(8,128)(2,1)} all-gather(bf16[16,1024]{1,0:T(8,128)(2,1)S(1)} %fusion.69), channel_id=2, replica_groups=mesh['seq'=32,'expert'=16] {'expert'}, dimensions={0}, use_global_device_ids=true | all-gather | bytes 557056 | tf_op jit(solution)/shard_map/all_gather | solution.py:100
  342.8 1.2 fusion.70
  344.0 2.8 fusion.17
  346.8 125.3 %all-reduce.8 = (bf16[16,1,2048]{2,0,1:T(8,128)(2,1)S(1)}, bf16[16,1,2048]{2,0,1:T(8,128)(2,1)S(1)}) all-reduce(f32[16,1,2048]{2,0,1:T(8,128)S(1)} %fusion.14, f32[16,1,2048]{2,0,1:T(8,128)S(1)} %fusion.17), channel_id=1, replica_groups=mesh['seq'=32,'expert'=16] {'seq'}, use_global_device_ids=true, to_apply=%region_6.0 | all-reduce | flops 65536 | bytes 393216 | tf_op jit(solution)/shard_map/psum | solution.py:20
  472.8 1.1 fusion.13
  473.9 0.9 convolution_convert_fusion.2
  474.8 1.1 fusion.12
  475.9 118.2 %all-reduce.7.cloned.1.call-done = bf16[16,2048]{1,0:T(8,128)(2,1)} async-done(((bf16[16,2048]{1,0:T(8,128)(2,1)}), bf16[16,2048]{1,0:T(8,128)(2,1)}) %all-reduce.7.cloned.1.call-update) | async-done | bytes 65552 | tf_op jit(solution)/shard_map/psum | solution.py:60
  594.2 3.6 fusion.40
  597.7 126.6 %all-reduce.9 = (bf16[16,2048]{1,0:T(8,128)(2,1)S(1)}, f32[16]{0:T(128)S(1)}) all-reduce(f32[16,2048]{1,0:T(8,128)S(1)} %fusion.34, f32[16]{0:T(128)S(1)} %get-tuple-element.13), channel_id=1, replica_groups=mesh['seq'=32,'expert'=16] {'seq'}, use_global_device_ids=true, to_apply=%region_7.0 | all-reduce | flops 32784 | bytes 196736 | tf_op jit(solution)/shard_map/psum | solution.py:30
  724.3 3.4 fusion.39
  727.7 29.1 %psum.62 = f32[1024]{0:T(1024)S(1)} all-reduce(f32[1024]{0:T(1024)S(1)} %get-tuple-element.15), channel_id=1, replica_groups=mesh['seq'=32,'expert'=16] {'expert'}, use_global_device_ids=true, to_apply=%region_13.0 | all-reduce | flops 1024 | bytes 8192 | tf_op jit(solution)/shard_map/psum | solution.py:88
  758.2 12.3 %reduce.11 = bf16[2048,16]{1,0:T(8,128)(2,1)} reduce(bf16[2048,1,16]{2,1,0:T(2,128)(2,1)S(1)} %bitcast.142, bf16[]{:T(256)} %broadcast.340), dimensions={1}, to_apply=%bitcast.124.reduce_sub_computation | reduce | bytes 131074
  770.5 2.2 reshape.132
  772.7 11.3 %all-to-all-start.1 = ((bf16[16,2,1024]{2,1,0:T(2,128)(2,1)}), bf16[16,2,1024]{2,1,0:T(2,128)(2,1)S(1)}, u32[]{:S(2)}, u32[]{:S(2)}) async-start(bf16[16,2,1024]{2,1,0:T(2,128)(2,1)} %reshape.132), calls=%async_computation.1 | async-start | bytes 131072 | tf_op jit(solution)/shard_map/all_to_all | solution.py:103
  784.0 0.9 fusion.42
  784.9 2.8 fusion.4
  788.5 11.6 %reduce.10 = bf16[2048,16]{1,0:T(8,128)(2,1)S(1)} reduce(bf16[2048,1,16]{2,1,0:T(2,128)(2,1)S(1)} %bitcast.143, bf16[]{:T(256)} %broadcast.340), dimensions={1}, to_apply=%bitcast.122.reduce_sub_computation | reduce | bytes 131074
  800.1 1.2 reshape.130
  801.3 124.4 %all-reduce.10 = bf16[16,2048]{1,0:T(8,128)(2,1)} all-reduce(f32[16,2048]{1,0:T(8,128)S(1)} %fusion.4), channel_id=1, replica_groups=mesh['seq'=32,'expert'=16] {'seq'}, use_global_device_ids=true, to_apply=%region_14.0 | all-reduce | flops 32768 | bytes 196608 | tf_op jit(solution)/shard_map/psum | solution.py:98
  925.7 12.0 %all-to-all-start = ((bf16[16,2,1024]{2,1,0:T(2,128)(2,1)}), bf16[16,2,1024]{2,1,0:T(2,128)(2,1)S(1)}, u32[]{:S(2)}, u32[]{:S(2)}) async-start(bf16[16,2,1024]{2,1,0:T(2,128)(2,1)} %reshape.130), calls=%async_computation | async-start | bytes 131072 | tf_op jit(solution)/shard_map/all_to_all | solution.py:32
  937.7 30.6 %all_gather.19 = bf16[256,1,1024]{2,0,1:T(8,128)(2,1)S(1)} all-gather(bf16[16,1,1024]{2,0,1:T(8,128)(2,1)S(1)} %fusion.42), channel_id=1, replica_groups=mesh['seq'=32,'expert'=16] {'expert'}, dimensions={0}, use_global_device_ids=true | all-gather | bytes 557056 | tf_op jit(solution)/shard_map/all_gather | solution.py:101
  968.3 0.9 reshape.133
  969.8 0.9 reshape.131
  971.3 1.1 fusion.22
  972.7 1.9 fusion.21
  (36 shorter events, 6.9 us)
Async XLA Ops:
  7.2 465.1 %copy-start = (bf16[1,128,2048]{2,1,0:T(8,128)(2,1)S(1)}, bf16[1,128,2048]{2,1,0:T(8,128)(2,1)}, u32[]{:S(2)}) copy-start(bf16[1,128,2048]{2,1,0:T(8,128)(2,1)} %param.8) | copy-start | bytes 1572868
  7.2 76.7 %all-gather.5.cloned.1.call-start = ((), (), s32[]{:S(2)}) async-start(), calls=%async_computation.2 | async-start | bytes 1114112 | tf_op jit(solution)/shard_map/all_gather | solution.py:71
  7.9 170.1 %all-gather.7.cloned.1.call-start = ((), (), s32[]{:S(2)}) async-start(), calls=%async_computation.3 | async-start | bytes 4456448 | tf_op jit(solution)/shard_map/all_gather | solution.py:70
  8.7 335.3 %all-gather.9.cloned.1.call-start = ((), (), s32[]{:S(2)}) async-start(), calls=%async_computation.4 | async-start | bytes 4456448 | tf_op jit(solution)/shard_map/all_gather | solution.py:80
  9.4 584.8 %all-reduce.7.cloned.1.call-start = ((), (), s32[]{:S(2)}) async-start(), calls=%async_computation.5 | async-start | bytes 131072 | tf_op jit(solution)/shard_map/psum | solution.py:60
  310.4 161.7 %copy-start.1 = (bf16[1,2048,128]{2,1,0:T(8,128)(2,1)S(1)}, bf16[1,2048,128]{2,1,0:T(8,128)(2,1)}, u32[]{:S(2)}) copy-start(bf16[1,2048,128]{2,1,0:T(8,128)(2,1)} %param.7) | copy-start | bytes 1572868
  594.2 162.7 %copy-start.3 = (bf16[16,2048]{1,0:T(8,128)(2,1)S(1)}, bf16[16,2048]{1,0:T(8,128)(2,1)}, u32[]{:S(2)}) copy-start(bf16[16,2048]{1,0:T(8,128)(2,1)} %all-reduce.7.cloned.1.call-done) | copy-start | bytes 196612
  772.7 153.0 %all-to-all-start.1 = ((bf16[16,2,1024]{2,1,0:T(2,128)(2,1)}), bf16[16,2,1024]{2,1,0:T(2,128)(2,1)S(1)}, u32[]{:S(2)}, u32[]{:S(2)}) async-start(bf16[16,2,1024]{2,1,0:T(2,128)(2,1)} %reshape.132), calls=%async_computation.1 | async-start | bytes 131072 | tf_op jit(solution)/shard_map/all_to_all | solution.py:103
  788.5 183.8 %copy-start.2 = (bf16[256,1024]{1,0:T(8,128)(2,1)S(1)}, bf16[256,1024]{1,0:T(8,128)(2,1)}, u32[]{:S(2)}) copy-start(bf16[256,1024]{1,0:T(8,128)(2,1)} %all-gather) | copy-start | bytes 1572868
  925.7 44.1 %all-to-all-start = ((bf16[16,2,1024]{2,1,0:T(2,128)(2,1)}), bf16[16,2,1024]{2,1,0:T(2,128)(2,1)S(1)}, u32[]{:S(2)}, u32[]{:S(2)}) async-start(bf16[16,2,1024]{2,1,0:T(2,128)(2,1)} %reshape.130), calls=%async_computation | async-start | bytes 131072 | tf_op jit(solution)/shard_map/all_to_all | solution.py:32
Sparse Core Ops, SparseCore 0:
  10.1 73.7 all-gather.4
  85.8 92.0 all-gather.6
  180.0 91.6 all-gather.8
  474.9 119.1 all-reduce.6
where the time goes:
time: 983 us; the launch traced here: 981 us
  blocking collectives  594 us (60%)
  waiting for transfers between devices  289 us (29%)
  other arithmetic  26.6 us (3%)
  matrix products  26.4 us (3%)
  starting transfers between devices  23.5 us (2%)
  between operations  13.9 us (1%)
    psum x1, blocking collectives, expert_forward(): expert_out = lax.psum(expert_part, 'seq')  127 us
    psum x1, blocking collectives, soft_dispatch(): slot_in = lax.psum(slot_partial, 'seq')  125 us
    psum x1, blocking collectives, local(): param_grad = lax.psum(param_part, 'seq').astype(bfloat)  124 us
    psum x1, waiting for transfers between devices, expert_backward(): input_grad = lax.psum(input_part.astype(jnp.bfloat16), 'seq')  118 us
    all_gather x1, waiting for transfers between devices, local(): features = lax.all_gather(tokens, 'expert', axis=2, tiled=True)  94.1 us
    all_gather x1, waiting for transfers between devices, local(): param_rows = lax.all_gather(slot_params, 'expert', axis=0, tiled=True)  74.4 us
    psum x1, blocking collectives, soft_dispatch(): denominator = lax.psum(jnp.sum(raised, axis=2), 'seq')  62.7 us
    pmax x1, blocking collectives, soft_dispatch(): maximum = lax.pmax(jnp.max(logits, axis=2), 'seq')  62.7 us
  transfers between devices with their start and end apart: 6, of which 3 were waited for; matrix products, arithmetic and copies ran while one was open for 3% of the time, Pallas kernels for 0%

commit v1 on v0

v1 whole, which is shorter than its diff:
```python
import functools

import jax
import jax.numpy as jnp
from jax import lax
from jax.experimental import pallas as pl
from jax.experimental.pallas import tpu as pltpu
from jax.sharding import PartitionSpec as P

BF = jnp.bfloat16
F32 = jnp.float32
INTERPRET = False


def call(body, out_shape, *args):
    vmem, smem = (pl.BlockSpec(memory_space=kind) for kind in (pltpu.VMEM, pltpu.SMEM))
    return pl.pallas_call(
        body,
        out_shape=out_shape,
        in_specs=[smem if arg.dtype == jnp.int32 else vmem for arg in args],
        interpret=INTERPRET,
        compiler_params=pltpu.CompilerParams(vmem_limit_bytes=48 * 1024 * 1024),
    )(*args)


def shape(dims, kind):
    return jax.ShapeDtypeStruct(dims, kind)


def nt(a, b):
    return lax.dot_general(a, b, (((1,), (1,)), ((), ())), preferred_element_type=F32)


def tn(a, b):
    return lax.dot_general(a, b, (((0,), (0,)), ((), ())), preferred_element_type=F32)


def nn(a, b):
    return jnp.dot(a, b, preferred_element_type=F32)


def split3(value):
    high = value.astype(BF).astype(F32)
    rest = value - high
    mid = rest.astype(BF).astype(F32)
    return [high, mid, (rest - mid).astype(BF).astype(F32)]


def lanes(ref, rows=slice(None)):
    return jnp.concatenate([ref[f, rows, :] for f in range(16)], axis=1)


def tokens_of(z_ref):
    count = (z_ref.shape[1] - 8) // 2
    return lanes(z_ref, slice(0, count)), lanes(z_ref, slice(count, 2 * count))


def route_kernel(pown_ref, pother_ref, z_ref, own_ref, other_ref, logit_ref, comb_ref):
    x, g = tokens_of(z_ref)
    logits = jnp.concatenate([nt(x, lanes(ref)) for ref in (pown_ref, pother_ref)], axis=1)
    logit_ref[...] = logits
    peak = jnp.max(logits, axis=0, keepdims=True)
    raised = jnp.exp(logits - peak)
    total = jnp.sum(raised, axis=0, keepdims=True)
    lifted = jnp.exp(logits - jnp.max(logits, axis=1, keepdims=True))
    combine = lifted / jnp.sum(lifted, axis=1, keepdims=True)
    comb_ref[...] = combine
    stats = jnp.concatenate(
        split3(peak) + split3(total) + [jnp.zeros((10, 256), F32)], axis=0
    ).astype(BF)
    for pay_ref, cols in ((own_ref, slice(0, 128)), (other_ref, slice(128, 256))):
        part_in = tn(raised[:, cols].astype(BF), x).astype(BF)
        part_grad = tn(combine[:, cols].astype(BF), g).astype(BF)
        for f in range(16):
            feats = slice(f * 128, (f + 1) * 128)
            pay_ref[f, 0:128, :] = part_in[:, feats]
            pay_ref[f, 128:256, :] = part_grad[:, feats]
            pay_ref[f, 256:272, :] = stats[:, cols]


def rescale(stats):
    peaks = jnp.concatenate([s[0:1] + s[1:2] + s[2:3] for s in stats], axis=0)
    totals = jnp.concatenate([s[3:4] + s[4:5] + s[5:6] for s in stats], axis=0)
    peak = jnp.max(peaks, axis=0, keepdims=True)
    scale = jnp.exp(peaks - peak)
    total = jnp.sum(scale * totals, axis=0, keepdims=True)
    rows = split3(peak) + split3(total)
    pad = jnp.zeros((122 - len(stats), 128), F32)
    return rows, jnp.concatenate([scale] + rows + [pad], axis=0).T


def merge_core_kernel(own_ref, sib_ref, pay_ref):
    rows, columns = rescale([ref[0, 256:272, :].astype(F32) for ref in (own_ref, sib_ref)])
    stats = jnp.concatenate(rows + [jnp.zeros((10, 128), F32)], axis=0).astype(BF)
    for f in range(16):
        pay_ref[f, 0:128, :] = (
            columns[:, 0:1] * own_ref[f, 0:128, :].astype(F32)
            + columns[:, 1:2] * sib_ref[f, 0:128, :].astype(F32)
        ).astype(BF)
        pay_ref[f, 128:256, :] = (
            own_ref[f, 128:256, :].astype(F32) + sib_ref[f, 128:256, :].astype(F32)
        ).astype(BF)
        pay_ref[f, 256:272, :] = stats


def merge_seq_kernel(r_ref, pay_ref):
    rows, columns = rescale([r_ref[i, 256:272, :].astype(F32) for i in range(16)])
    sum_in = jnp.zeros((128, 128), F32)
    sum_grad = jnp.zeros((128, 128), F32)
    for i in range(16):
        sum_in = sum_in + columns[:, i : i + 1] * r_ref[i, 0:128, :].astype(F32)
        sum_grad = sum_grad + r_ref[i, 128:256, :].astype(F32)
    for e in range(16):
        rows = slice(e * 8, (e + 1) * 8)
        pay_ref[e] = jnp.concatenate(
            [sum_in[rows], sum_grad[rows], columns[rows]], axis=0
        ).astype(BF)


def merge_expert_kernel(r_ref, pay_ref, slot_ref, log_ref):
    blocks = [r_ref[i].astype(F32) for i in range(16)]
    peaks = [b[16:24, 16:17] + b[16:24, 17:18] + b[16:24, 18:19] for b in blocks]
    totals = [b[16:24, 19:20] + b[16:24, 20:21] + b[16:24, 21:22] for b in blocks]
    peak = functools.reduce(jnp.maximum, peaks)
    slot = jnp.zeros((8, 128), F32)
    grad = jnp.zeros((8, 128), F32)
    total = jnp.zeros((8, 1), F32)
    for i in range(16):
        scale = jnp.exp(peaks[i] - peak)
        slot = slot + scale * blocks[i][0:8]
        total = total + scale * totals[i]
        grad = grad + blocks[i][8:16]
    slot = slot / total
    slot_ref[...] = slot
    log_ref[...] = jnp.broadcast_to(peak + jnp.log(total), (8, 128))
    both = jnp.concatenate([slot, grad], axis=0).astype(BF)
    for i in range(32):
        pay_ref[i] = both


def expert_kernel(r_ref, win_ref, wout_ref, pay_ref, slot_ref, grad_ref, hidden_ref, pre_ref):
    blocks = [r_ref[i].astype(F32) for i in range(32)]

    def rows(first):
        return jnp.concatenate(
            [
                jnp.concatenate(
                    [blocks[2 * f][first : first + 8], blocks[2 * f + 1][first : first + 8]],
                    axis=0,
                )
                for f in range(16)
            ],
            axis=1,
        ).astype(BF)

    slot, grad = rows(0), rows(8)
    preact = nn(slot, win_ref[...])
    cdf = 0.5 * (1.0 + lax.erf(preact * 0.7071067811865476))
    density = 0.3989422804014327 * jnp.exp(-0.5 * preact * preact)
    hidden = (preact * cdf).astype(BF)
    hidden_grad = nt(grad, wout_ref[...])
    pre = (hidden_grad * (cdf + preact * density)).astype(BF)
    out_part = nn(hidden, wout_ref[...])
    in_part = nt(pre, win_ref[...])
    for h in range(2):
        for f in range(16):
            rows_, feats = slice(h * 8, h * 8 + 8), slice(f * 128, (f + 1) * 128)
            pay_ref[f * 2 + h] = jnp.concatenate(
                [out_part[rows_, feats], in_part[rows_, feats]], axis=0
            ).astype(BF)
    slot_ref[...] = slot
    grad_ref[...] = grad
    hidden_ref[...] = hidden
    pre_ref[...] = pre


def out_merge_kernel(r_ref, slot_ref, log_ref, pay_ref):
    both = functools.reduce(jnp.add, [r_ref[i].astype(F32) for i in range(32)])
    both = both.astype(BF).astype(F32)
    guess = jnp.sum(both[8:16] * slot_ref[...], axis=1, keepdims=True)
    lane = lax.broadcasted_iota(jnp.int32, (8, 128), 1)
    stats = jnp.zeros((8, 128), F32)
    for at, value in enumerate(split3(log_ref[...][:, 0:1]) + split3(guess)):
        stats = jnp.where(lane == at, value, stats)
    both = jnp.concatenate([both, stats], axis=0).astype(BF)
    for i in range(16):
        pay_ref[i] = both


def spread_kernel(r_ref, pay_ref):
    blocks = [r_ref[i].astype(F32) for i in range(16)]
    out = jnp.concatenate([b[0:8] for b in blocks], axis=0).astype(BF)
    inp = jnp.concatenate([b[8:16] for b in blocks], axis=0).astype(BF)
    stats = jnp.concatenate([b[16:24] for b in blocks], axis=0).T[0:16].astype(BF)
    for i in range(16):
        pay_ref[i, 0:128, :] = out
        pay_ref[i, 128:256, :] = inp
        pay_ref[i, 256:272, :] = stats


def mix_kernel(
    own_ref, other_ref, z_ref, logit_ref, comb_ref,
    mixed_ref, parown_ref, parother_ref, guess_ref, disp_ref, cot_ref, term_ref, in_ref,
):
    x, g = tokens_of(z_ref)
    combine = comb_ref[...]
    combine_low = combine.astype(BF)
    pair = (own_ref, other_ref)
    stats = [ref[0, 256:272, :].astype(F32) for ref in pair]
    logs = jnp.concatenate([s[0:1] + s[1:2] + s[2:3] for s in stats], axis=1)
    sums = [
        functools.reduce(jnp.add, [ref[f, 256:272, :].astype(F32) for f in range(16)])
        for ref in pair
    ]
    guess = jnp.concatenate([s[3:4] + s[4:5] + s[5:6] for s in sums], axis=1)
    outs = jnp.concatenate([lanes(ref, slice(0, 128)) for ref in pair], axis=0)
    ins = jnp.concatenate([lanes(ref, slice(128, 256)) for ref in pair], axis=0)
    dispatch_cot = nt(x, ins)
    dispatch = jnp.exp(logit_ref[...] - logs)
    column = jnp.sum(dispatch.astype(BF).astype(F32) * dispatch_cot, axis=0, keepdims=True)
    combine_cot = nt(g, outs)
    row_sum = jnp.sum(combine_low.astype(F32) * combine_cot, axis=1, keepdims=True)
    term = combine * (combine_cot - row_sum)
    logit_low = (dispatch * (dispatch_cot - guess) + term).astype(BF)
    for ref, half in ((parown_ref, slice(0, 128)), (parother_ref, slice(128, 256))):
        part = tn(logit_low[:, half], x).astype(BF)
        sums = jnp.concatenate(
            split3(column[:, half]) + [jnp.zeros((13, 128), F32)], axis=0
        ).astype(BF)
        for f in range(16):
            ref[f, 0:128, :] = part[:, f * 128 : (f + 1) * 128]
            ref[f, 128:144, :] = sums
    mixed = nn(combine_low, outs).astype(BF)
    for f in range(16):
        mixed_ref[f] = mixed[:, f * 128 : (f + 1) * 128]
    guess_ref[...] = jnp.broadcast_to(guess, (8, 256))
    disp_ref[...] = dispatch
    cot_ref[...] = dispatch_cot
    term_ref[...] = term
    in_ref[...] = ins


def column_of(block):
    return block[0:1] + block[1:2] + block[2:3]


def param_core_kernel(own_ref, sib_ref, pay_ref):
    sums = [ref[0, 128:144, :].astype(F32) for ref in (own_ref, sib_ref)]
    sums = jnp.concatenate(
        split3(column_of(sums[0]) + column_of(sums[1])) + [jnp.zeros((13, 128), F32)], axis=0
    ).astype(BF)
    for f in range(16):
        pay_ref[f, 0:128, :] = (
            own_ref[f, 0:128, :].astype(F32) + sib_ref[f, 0:128, :].astype(F32)
        ).astype(BF)
        pay_ref[f, 128:144, :] = sums


def param_seq_kernel(r_ref, mixed_ref, pay_ref):
    count = mixed_ref.shape[1]
    total = functools.reduce(jnp.add, [r_ref[i, 0:128, :].astype(F32) for i in range(16)])
    column = functools.reduce(
        jnp.add, [column_of(r_ref[i, 128:144, :].astype(F32)) for i in range(16)]
    )
    sums = jnp.concatenate(split3(column) + [jnp.zeros((5, 128), F32)], axis=0)
    for e in range(16):
        pay_ref[e, 0:count, :] = mixed_ref[e]
        pay_ref[e, count : count + 16, :] = jnp.concatenate(
            [total[e * 8 : (e + 1) * 8], sums], axis=0
        ).astype(BF)


def param_expert_kernel(at_ref, r_ref, guess_ref, slot_ref, pay_ref, col_ref):
    count = r_ref.shape[1] - 16
    total = functools.reduce(
        jnp.add, [r_ref[i, count : count + 16, :].astype(F32) for i in range(16)]
    )
    column = column_of(total[8:16])
    col_ref[...] = jnp.broadcast_to(column, (8, 128))
    missed = column - guess_ref[0:1, 0:128]
    lane = lax.broadcasted_iota(jnp.int32, (8, 128), 1)
    row = lax.broadcasted_iota(jnp.int32, (8, 128), 0)
    missed = jnp.sum(
        jnp.where(lane == at_ref[0] * 8 + row, missed, 0.0), axis=1, keepdims=True
    )
    param = total[0:8] - missed * slot_ref[...]
    for i in range(32):
        pay_ref[i] = param


def token_kernel(
    colown_ref, colother_ref, pown_ref, pother_ref, disp_ref, cot_ref, term_ref, in_ref, tok_ref
):
    column = jnp.concatenate([colown_ref[0:1, :], colother_ref[0:1, :]], axis=1)
    params = jnp.concatenate([lanes(pown_ref), lanes(pother_ref)], axis=0)
    dispatch = disp_ref[...]
    logit_low = (dispatch * (cot_ref[...] - column) + term_ref[...]).astype(BF)
    token_grad = (nn(dispatch.astype(BF), in_ref[...]) + nn(logit_low, params)).astype(BF)
    for f in range(16):
        tok_ref[f] = token_grad[:, f * 128 : (f + 1) * 128]


CHIPS = [list(range(0, 32, 2)), list(range(1, 32, 2))]
SIBLING = [(i, i ^ 1) for i in range(32)]


def swap(array, axis, groups=None):
    return lax.all_to_all(
        array, axis, split_axis=0, concat_axis=0, tiled=True, axis_index_groups=groups
    )


def local(tokens, slot_params, w_in, w_out, out_grad):
    count = tokens.shape[1] // 16
    seq_at = lax.axis_index("seq")
    expert_at = lax.axis_index("expert").astype(jnp.int32).reshape(1)
    piece = lax.dynamic_slice(
        slot_params, ((seq_at % 2) * 8, (seq_at // 2) * 128), (8, 128)
    )
    block = jnp.concatenate(
        [
            tokens.reshape(16, count, 128),
            out_grad.reshape(16, count, 128),
            jnp.broadcast_to(piece[None], (16, 8, 128)),
        ],
        axis=1,
    )
    z = swap(block, "expert")
    mine = z[:, 2 * count :].reshape(128, 128)
    params = swap(jnp.broadcast_to(mine[None], (16, 128, 128)), "seq", CHIPS)
    params_other = lax.ppermute(params, "seq", SIBLING)

    half = shape((16, 272, 128), BF)
    slots = shape((count, 256), F32)
    small = shape((16, 24, 128), BF)
    row = shape((8, 128), F32)
    own, other, logits, combine = call(
        route_kernel, (half, half, slots, slots), params, params_other, z
    )
    sibling = lax.ppermute(other, "seq", SIBLING)
    pay = call(merge_core_kernel, half, own, sibling)
    pay = call(merge_seq_kernel, small, swap(pay, "seq", CHIPS))
    pay, slot_piece, log_piece = call(
        merge_expert_kernel, (shape((32, 16, 128), BF), row, row), swap(pay, "expert")
    )
    pay, slot_low, grad_low, hidden, pre = call(
        expert_kernel,
        (
            shape((32, 16, 128), BF),
            shape((16, 2048), BF),
            shape((16, 2048), BF),
            shape((16, 128), BF),
            shape((16, 128), BF),
        ),
        swap(pay, "seq"),
        w_in[0],
        w_out[0],
    )
    w_out_grad = tn(hidden, grad_low).astype(BF)
    w_in_grad = tn(slot_low, pre).astype(BF)
    pay = call(out_merge_kernel, small, swap(pay, "seq"), slot_piece, log_piece)
    pay = call(spread_kernel, half, swap(pay, "expert"))
    own = swap(pay, "seq", CHIPS)
    other = lax.ppermute(own, "seq", SIBLING)
    part = shape((16, 144, 128), BF)
    by_feature = shape((16, count, 128), BF)
    mixed, own, other, guess, dispatch, dispatch_cot, term, ins = call(
        mix_kernel,
        (
            by_feature, part, part, shape((8, 256), F32),
            slots, slots, slots, shape((256, 2048), BF),
        ),
        own,
        other,
        z,
        logits,
        combine,
    )
    pay = call(param_core_kernel, part, own, lax.ppermute(other, "seq", SIBLING))
    pay = call(
        param_seq_kernel, shape((16, count + 16, 128), BF), swap(pay, "seq", CHIPS), mixed
    )
    pay = swap(pay, "expert")
    mixed = pay[:, 0:count].reshape(tokens.shape)
    param_grad, column = call(
        param_expert_kernel, (shape((32, 8, 128), F32), row), expert_at, pay, guess, slot_piece
    )
    token_grad = call(
        token_kernel,
        by_feature,
        column,
        lax.ppermute(column, "seq", SIBLING),
        params,
        params_other,
        dispatch,
        dispatch_cot,
        term,
        ins,
    )
    token_grad = swap(token_grad, "expert").reshape(tokens.shape)
    param_grad = swap(param_grad, "seq")
    param_grad = (
        param_grad.reshape(16, 2, 8, 128).transpose(1, 2, 0, 3).reshape(16, 2048).astype(BF)
    )
    return (mixed, token_grad, param_grad, w_in_grad[None], w_out_grad[None])


def solution(mesh):
    return jax.shard_map(
        local,
        mesh=mesh,
        in_specs=(
            P(None, "seq", "expert"),
            P("expert", None),
            P("expert", None, "seq"),
            P("expert", "seq", None),
            P(None, "seq", "expert"),
        ),
        out_specs=(
            P(None, "seq", "expert"),
            P(None, "seq", "expert"),
            P("expert", None),
            P("expert", None, "seq"),
            P("expert", "seq", None),
        ),
        check_vma=False,
    )
```

time: 983 us -> 267 us (0.27)
  the two profiles are of different devices: /device:TPU:64 before, /device:TPU:32 now
where the time goes in v1:
time: 267 us
  blocking collectives  178 us (67%)
  waiting for transfers between devices  47.8 us (18%)
  starting transfers between devices  25.7 us (10%)
  Pallas kernels  7.22 us (3%)
  local copies, waits for them, and re-layouts  2.87 us (1%)
    all_to_all x9, blocking collectives, swap(): lax.all_to_all(array, axis, split_axis=0, concat_axis=0, tiled=True, axis...  178 us
    all_to_all x3, waiting for transfers between devices, swap(): lax.all_to_all(array, axis, split_axis=0, concat_axis=0, tiled=True, axis...  37.9 us
    all_to_all x3, starting transfers between devices, swap(): lax.all_to_all(array, axis, split_axis=0, concat_axis=0, tiled=True, axis...  15.6 us
    pallas_call x12, Pallas kernels, call(): pl.pallas_call(body, out_shape=out_shape, in_specs=[smem if arg.dtype ==...  7.22 us
  transfers between devices with their start and end apart: 8, of which 8 were waited for; matrix products, arithmetic and copies ran while one was open for 1% of the time, Pallas kernels for 0%

profile of v1, /device:TPU:32, one launch (start us, length us, event | category | flops | bytes accessed | tf_op | source)
XLA Modules:
  0.0 266.6 jit_solution(17432408056896680744)
XLA Ops:
  1.4 1.1 pad_maximum_fusion
  2.4 48.1 %all_to_all.60.z_ref = bf16[16,136,128]{2,1,0:T(8,128)(2,1)S(1)} all-to-all(bf16[16,136,128]{2,1,0:T(8,128)(2,1)S(1)} %pad_maximum_fusion), channel_id=1, replica_groups=mesh['seq'=32,'expert'=16] {'expert'}, dimensions={0} | all-to-all | bytes 1114112 | tf_op jit(solution)/shard_map/all_to_all | solution.py:308
  50.6 17.2 %all_to_all.61.pown_ref = bf16[16,128,128]{2,1,0:T(8,128)(2,1)S(1)} all-to-all(bf16[16,128,128]{2,1,0:T(8,128)(2,1)S(1)} %broadcast_in_dim.21), channel_id=1, replica_groups={{0,32,64,96,128,160,192,224,256,288,320,352,384,416,448,480},{16,48,80,..., dimensions={0} | all-to-all | bytes 1048576 | tf_op jit(solution)/shard_map/all_to_all | solution.py:308
  67.8 1.9 collective-permute-start
  69.7 1.9 collective-permute-done.pother_ref
  71.6 1.3 shard_map.92
  72.9 2.0 collective-permute-start.1
  75.0 2.6 collective-permute-done.1.sib_ref
  78.1 21.4 %all_to_all.62.r_ref = bf16[16,272,128]{2,1,0:T(8,128)(2,1)S(1)} all-to-all(bf16[16,272,128]{2,1,0:T(8,128)(2,1)S(1)} %shard_map.93), channel_id=1, replica_groups={{0,32,64,96,128,160,192,224,256,288,320,352,384,416,448,480},{16,48,80,..., dimensions={0} | all-to-all | bytes 2228224 | tf_op jit(solution)/shard_map/all_to_all | solution.py:308
  100.0 16.7 %all_to_all.63.r_ref = bf16[16,24,128]{2,1,0:T(8,128)(2,1)S(1)} all-to-all(bf16[16,24,128]{2,1,0:T(8,128)(2,1)S(1)} %shard_map.94), channel_id=1, replica_groups=mesh['seq'=32,'expert'=16] {'expert'}, dimensions={0} | all-to-all | bytes 196608 | tf_op jit(solution)/shard_map/all_to_all | solution.py:308
  117.0 11.4 %all_to_all.64.r_ref = bf16[32,16,128]{2,1,0:T(8,128)(2,1)S(1)} all-to-all(bf16[32,16,128]{2,1,0:T(8,128)(2,1)S(1)} %get-tuple-element.29), channel_id=1, replica_groups=mesh['seq'=32,'expert'=16] {'seq'}, dimensions={0} | all-to-all | bytes 262144 | tf_op jit(solution)/shard_map/all_to_all | solution.py:308
  129.2 11.3 %all_to_all.65.r_ref = bf16[32,16,128]{2,1,0:T(8,128)(2,1)S(1)} all-to-all(bf16[32,16,128]{2,1,0:T(8,128)(2,1)S(1)} %get-tuple-element.30), channel_id=1, replica_groups=mesh['seq'=32,'expert'=16] {'seq'}, dimensions={0} | all-to-all | bytes 262144 | tf_op jit(solution)/shard_map/all_to_all | solution.py:308
  140.6 17.2 %all_to_all.66.r_ref = bf16[16,24,128]{2,1,0:T(8,128)(2,1)S(1)} all-to-all(bf16[16,24,128]{2,1,0:T(8,128)(2,1)S(1)} %shard_map.97), channel_id=1, replica_groups=mesh['seq'=32,'expert'=16] {'expert'}, dimensions={0} | all-to-all | bytes 196608 | tf_op jit(solution)/shard_map/all_to_all | solution.py:308
  157.9 19.1 %all_to_all.67.own_ref = bf16[16,272,128]{2,1,0:T(8,128)(2,1)S(1)} all-to-all(bf16[16,272,128]{2,1,0:T(8,128)(2,1)S(1)} %shard_map.98), channel_id=1, replica_groups={{0,32,64,96,128,160,192,224,256,288,320,352,384,416,448,480},{16,48,80,..., dimensions={0} | all-to-all | bytes 2228224 | tf_op jit(solution)/shard_map/all_to_all | solution.py:308
  177.1 1.9 collective-permute-start.2
  179.0 2.7 %collective-permute-done.2.other_ref = bf16[16,272,128]{2,1,0:T(8,128)(2,1)S(1)} collective-permute-done((bf16[16,272,128]{2,1,0:T(8,128)(2,1)S(1)}, bf16[16,272,128]{2,1,0:T(8,128)(2,1)S(1)}, u32[]{:S(2)}, u32[]{:S(2)}) %collective-permute-start.2) | collective-permute-done | bytes 1114144 | tf_op jit(solution)/shard_map/ppermute | solution.py:364
  181.7 1.4 shard_map.99
  183.1 2.0 collective-permute-start.3
  185.2 1.8 collective-permute-done.3.sib_ref
  187.2 15.8 %all_to_all.68.r_ref = bf16[16,144,128]{2,1,0:T(8,128)(2,1)S(1)} all-to-all(bf16[16,144,128]{2,1,0:T(8,128)(2,1)S(1)} %shard_map.100), channel_id=1, replica_groups={{0,32,64,96,128,160,192,224,256,288,320,352,384,416,448,480},{16,48,80,..., dimensions={0} | all-to-all | bytes 1179648 | tf_op jit(solution)/shard_map/all_to_all | solution.py:308
  203.0 0.8 shard_map.101
  203.8 5.7 %all-to-all-start.9 = ((bf16[16,80,128]{2,1,0:T(8,128)(2,1)}), bf16[16,80,128]{2,1,0:T(8,128)(2,1)S(1)}, u32[]{:S(2)}, u32[]{:S(2)}) async-start(bf16[16,80,128]{2,1,0:T(8,128)(2,1)} %shard_map.101), calls=%async_computation.9 | async-start | bytes 655360 | tf_op jit(solution)/shard_map/all_to_all | solution.py:308
  209.4 19.9 %all-to-all-done.9.r_ref = bf16[16,80,128]{2,1,0:T(8,128)(2,1)S(1)} async-done(((bf16[16,80,128]{2,1,0:T(8,128)(2,1)}), bf16[16,80,128]{2,1,0:T(8,128)(2,1)S(1)}, u32[]{:S(2)}, u32[]{:S(2)}) %all-to-all-start.9) | async-done | bytes 327712 | tf_op jit(solution)/shard_map/all_to_all | solution.py:308
  230.1 4.2 %all-to-all-start.11 = ((bf16[32,8,128]{2,1,0:T(8,128)(2,1)}), bf16[32,8,128]{2,1,0:T(8,128)(2,1)S(1)}, u32[]{:S(2)}, u32[]{:S(2)}) async-start(bf16[32,8,128]{2,1,0:T(8,128)(2,1)} %convert), calls=%async_computation.11 | async-start | bytes 131072 | tf_op jit(solution)/shard_map/all_to_all | solution.py:308
  234.3 2.2 collective-permute-start.4
  236.5 0.9 collective-permute-done.4.colother_ref
  237.4 1.2 shard_map.103
  238.6 3.3 %all-to-all-done.11 = bf16[32,8,128]{2,1,0:T(8,128)(2,1)S(1)} async-done(((bf16[32,8,128]{2,1,0:T(8,128)(2,1)}), bf16[32,8,128]{2,1,0:T(8,128)(2,1)S(1)}, u32[]{:S(2)}, u32[]{:S(2)}) %all-to-all-start.11) | async-done | bytes 65568 | tf_op jit(solution)/shard_map/all_to_all | solution.py:308
  241.8 5.7 %all-to-all-start.10 = ((bf16[16,64,128]{2,1,0:T(8,128)(2,1)}), bf16[16,64,128]{2,1,0:T(8,128)(2,1)S(1)}, u32[]{:S(2)}, u32[]{:S(2)}) async-start(bf16[16,64,128]{2,1,0:T(8,128)(2,1)} %shard_map.103), calls=%async_computation.10 | async-start | bytes 524288 | tf_op jit(solution)/shard_map/all_to_all | solution.py:308
  247.6 1.1 fusion
  248.7 1.1 fusion.1
  251.2 14.7 %all-to-all-done.10 = bf16[16,64,128]{2,1,0:T(8,128)(2,1)S(1)} async-done(((bf16[16,64,128]{2,1,0:T(8,128)(2,1)}), bf16[16,64,128]{2,1,0:T(8,128)(2,1)S(1)}, u32[]{:S(2)}, u32[]{:S(2)}) %all-to-all-start.10) | async-done | bytes 262176 | tf_op jit(solution)/shard_map/all_to_all | solution.py:308
  (20 shorter events, 6.0 us)
Async XLA Ops:
  67.8 3.8 %collective-permute-start = (bf16[16,128,128]{2,1,0:T(8,128)(2,1)S(1)}, bf16[16,128,128]{2,1,0:T(8,128)(2,1)S(1)}, u32[]{:S(2)}, u32[]{:S(2)}) collective-permute-start(bf16[16,128,128]{2,1,0:T(8,128)(2,1)S(1)} %all_to_all.61.pown_ref), channel_id=1, source_target_pairs={{0,16},{16,0},{32,48},{48,32},{64,80},{80,64},{96,112},{112,96},{1... | collective-permute-start | bytes 1572872 | tf_op jit(solution)/shard_map/ppermute | solution.py:331
  72.9 4.6 %collective-permute-start.1 = (bf16[16,272,128]{2,1,0:T(8,128)(2,1)S(1)}, bf16[16,272,128]{2,1,0:T(8,128)(2,1)S(1)}, u32[]{:S(2)}, u32[]{:S(2)}) collective-permute-start(bf16[16,272,128]{2,1,0:T(8,128)(2,1)S(1)} %get-tuple-element.28), channel_id=1, source_target_pairs={{0,16},{16,0},{32,48},{48,32},{64,80},{80,64},{96,112},{112,96},{1... | collective-permute-start | bytes 3342344 | tf_op jit(solution)/shard_map/ppermute | solution.py:340
  99.5 29.0 %copy-start = (bf16[1,2048,128]{2,1,0:T(8,128)(2,1)S(1)}, bf16[1,2048,128]{2,1,0:T(8,128)(2,1)}, u32[]{:S(2)}) copy-start(bf16[1,2048,128]{2,1,0:T(8,128)(2,1)} %param.7) | copy-start | bytes 1572868
  99.5 29.0 %copy-start.1 = (bf16[1,128,2048]{2,1,0:T(8,128)(2,1)S(1)}, bf16[1,128,2048]{2,1,0:T(8,128)(2,1)}, u32[]{:S(2)}) copy-start(bf16[1,128,2048]{2,1,0:T(8,128)(2,1)} %param.8) | copy-start | bytes 1572868
  177.1 4.6 %collective-permute-start.2 = (bf16[16,272,128]{2,1,0:T(8,128)(2,1)S(1)}, bf16[16,272,128]{2,1,0:T(8,128)(2,1)S(1)}, u32[]{:S(2)}, u32[]{:S(2)}) collective-permute-start(bf16[16,272,128]{2,1,0:T(8,128)(2,1)S(1)} %all_to_all.67.own_ref), channel_id=1, source_target_pairs={{0,16},{16,0},{32,48},{48,32},{64,80},{80,64},{96,112},{112,96},{1... | collective-permute-start | bytes 3342344 | tf_op jit(solution)/shard_map/ppermute | solution.py:364
  183.1 3.9 %collective-permute-start.3 = (bf16[16,144,128]{2,1,0:T(8,128)(2,1)S(1)}, bf16[16,144,128]{2,1,0:T(8,128)(2,1)S(1)}, u32[]{:S(2)}, u32[]{:S(2)}) collective-permute-start(bf16[16,144,128]{2,1,0:T(8,128)(2,1)S(1)} %get-tuple-element.36), channel_id=1, source_target_pairs={{0,16},{16,0},{32,48},{48,32},{64,80},{80,64},{96,112},{112,96},{1... | collective-permute-start | bytes 1769480 | tf_op jit(solution)/shard_map/ppermute | solution.py:379
  203.8 25.6 %all-to-all-start.9 = ((bf16[16,80,128]{2,1,0:T(8,128)(2,1)}), bf16[16,80,128]{2,1,0:T(8,128)(2,1)S(1)}, u32[]{:S(2)}, u32[]{:S(2)}) async-start(bf16[16,80,128]{2,1,0:T(8,128)(2,1)} %shard_map.101), calls=%async_computation.9 | async-start | bytes 655360 | tf_op jit(solution)/shard_map/all_to_all | solution.py:308
  230.1 11.7 %all-to-all-start.11 = ((bf16[32,8,128]{2,1,0:T(8,128)(2,1)}), bf16[32,8,128]{2,1,0:T(8,128)(2,1)S(1)}, u32[]{:S(2)}, u32[]{:S(2)}) async-start(bf16[32,8,128]{2,1,0:T(8,128)(2,1)} %convert), calls=%async_computation.11 | async-start | bytes 131072 | tf_op jit(solution)/shard_map/all_to_all | solution.py:308
  234.3 3.1 %collective-permute-start.4 = (f32[8,128]{1,0:T(8,128)S(1)}, f32[8,128]{1,0:T(8,128)S(1)}, u32[]{:S(2)}, u32[]{:S(2)}) collective-permute-start(f32[8,128]{1,0:T(8,128)S(1)} %get-tuple-element.39.colown_ref), channel_id=1, source_target_pairs={{0,16},{16,0},{32,48},{48,32},{64,80},{80,64},{96,112},{112,96},{1... | collective-permute-start | bytes 12296 | tf_op jit(solution)/shard_map/ppermute | solution.py:392
  241.8 24.1 %all-to-all-start.10 = ((bf16[16,64,128]{2,1,0:T(8,128)(2,1)}), bf16[16,64,128]{2,1,0:T(8,128)(2,1)S(1)}, u32[]{:S(2)}, u32[]{:S(2)}) async-start(bf16[16,64,128]{2,1,0:T(8,128)(2,1)} %shard_map.103), calls=%async_computation.10 | async-start | bytes 524288 | tf_op jit(solution)/shard_map/all_to_all | solution.py:308

commit v2 on v1

--- a/solution.py
+++ b/solution.py
@@ -50,14 +50,33 @@
     return jnp.concatenate([ref[f, rows, :] for f in range(16)], axis=1)
 
 
-def tokens_of(z_ref):
-    count = (z_ref.shape[1] - 8) // 2
-    return lanes(z_ref, slice(0, count)), lanes(z_ref, slice(count, 2 * count))
-
-
-def route_kernel(pown_ref, pother_ref, z_ref, own_ref, other_ref, logit_ref, comb_ref):
-    x, g = tokens_of(z_ref)
-    logits = jnp.concatenate([nt(x, lanes(ref)) for ref in (pown_ref, pother_ref)], axis=1)
+def chip_order(at_ref):
+    masks = [at_ref[1] ^ f for f in range(16)]
+    return [m ^ ((m >> 1) & 5) for m in masks]
+
+
+def stage_kernel(z_ref, g_ref, mine_ref, out_ref):
+    count = g_ref.shape[1]
+    blocks = [z_ref[f].astype(F32)[count:] for f in range(16)]
+    mine_ref[0] = jnp.concatenate(blocks, axis=0).astype(BF)
+    out_ref[...] = g_ref[...]
+
+
+def route_kernel(
+    at_ref, pown_ref, pother_ref, z_ref, g_ref, own_ref, other_ref, logit_ref, comb_ref, par_ref
+):
+    x = lanes(z_ref, slice(0, g_ref.shape[1]))
+    g = lanes(g_ref)
+    order = chip_order(at_ref)
+    params = jnp.concatenate(
+        [
+            jnp.concatenate([ref[j] for j in order], axis=1)
+            for ref in (pown_ref, pother_ref)
+        ],
+        axis=0,
+    )
+    par_ref[...] = params
+    logits = nt(x, params)
     logit_ref[...] = logits
     peak = jnp.max(logits, axis=0, keepdims=True)
     raised = jnp.exp(logits - peak)
@@ -199,10 +218,11 @@
 
 
 def mix_kernel(
-    own_ref, other_ref, z_ref, logit_ref, comb_ref,
+    own_ref, other_ref, z_ref, g_ref, logit_ref, comb_ref,
     mixed_ref, parown_ref, parother_ref, guess_ref, disp_ref, cot_ref, term_ref, in_ref,
 ):
-    x, g = tokens_of(z_ref)
+    x = lanes(z_ref, slice(0, g_ref.shape[1]))
+    g = lanes(g_ref)
     combine = comb_ref[...]
     combine_low = combine.astype(BF)
     pair = (own_ref, other_ref)
@@ -283,25 +303,40 @@
     missed = jnp.sum(
         jnp.where(lane == at_ref[0] * 8 + row, missed, 0.0), axis=1, keepdims=True
     )
-    param = total[0:8] - missed * slot_ref[...]
-    for i in range(32):
-        pay_ref[i] = param
+    pay_ref[0] = total[0:8] - missed * slot_ref[...]
 
 
 def token_kernel(
-    colown_ref, colother_ref, pown_ref, pother_ref, disp_ref, cot_ref, term_ref, in_ref, tok_ref
+    colown_ref, colother_ref, par_ref, disp_ref, cot_ref, term_ref, in_ref, grad_ref,
+    tok_ref, out_ref,
 ):
     column = jnp.concatenate([colown_ref[0:1, :], colother_ref[0:1, :]], axis=1)
-    params = jnp.concatenate([lanes(pown_ref), lanes(pother_ref)], axis=0)
     dispatch = disp_ref[...]
     logit_low = (dispatch * (cot_ref[...] - column) + term_ref[...]).astype(BF)
-    token_grad = (nn(dispatch.astype(BF), in_ref[...]) + nn(logit_low, params)).astype(BF)
+    token_grad = (nn(dispatch.astype(BF), in_ref[...]) + nn(logit_low, par_ref[...])).astype(BF)
     for f in range(16):
         tok_ref[f] = token_grad[:, f * 128 : (f + 1) * 128]
+    out_ref[...] = grad_ref[...]
+
+
+def param_out_kernel(at_ref, own_ref, other_ref, out_ref):
+    first = at_ref[2] == 0
+    for f, j in enumerate(chip_order(at_ref)):
+        own, other = own_ref[j], other_ref[j]
+        out_ref[:, f * 128 : (f + 1) * 128] = jnp.concatenate(
+            [jnp.where(first, own, other), jnp.where(first, other, own)], axis=0
+        ).astype(BF)
 
 
 CHIPS = [list(range(0, 32, 2)), list(range(1, 32, 2))]
 SIBLING = [(i, i ^ 1) for i in range(32)]
+
+
+def gather_chips(block):
+    for mask in (1, 3, 4, 12):
+        pairs = [(i, ((i // 2) ^ mask) * 2 + i % 2) for i in range(32)]
+        block = jnp.concatenate([block, lax.ppermute(block, "seq", pairs)], axis=0)
+    return block
 
 
 def swap(array, axis, groups=None):
@@ -313,29 +348,37 @@
 def local(tokens, slot_params, w_in, w_out, out_grad):
     count = tokens.shape[1] // 16
     seq_at = lax.axis_index("seq")
-    expert_at = lax.axis_index("expert").astype(jnp.int32).reshape(1)
+    at = jnp.stack([lax.axis_index("expert"), seq_at // 2, seq_at % 2]).astype(jnp.int32)
     piece = lax.dynamic_slice(
         slot_params, ((seq_at % 2) * 8, (seq_at // 2) * 128), (8, 128)
     )
+    by_feature = shape((16, count, 128), BF)
     block = jnp.concatenate(
-        [
-            tokens.reshape(16, count, 128),
-            out_grad.reshape(16, count, 128),
-            jnp.broadcast_to(piece[None], (16, 8, 128)),
-        ],
-        axis=1,
+        [tokens.reshape(by_feature.shape), jnp.broadcast_to(piece[None], (16, 8, 128))], axis=1
     )
     z = swap(block, "expert")
-    mine = z[:, 2 * count :].reshape(128, 128)
-    params = swap(jnp.broadcast_to(mine[None], (16, 128, 128)), "seq", CHIPS)
+    mine, g = call(
+        stage_kernel,
+        (shape((1, 128, 128), BF), by_feature),
+        z,
+        out_grad.reshape(by_feature.shape),
+    )
+    g = swap(g, "expert")
+    params = gather_chips(mine)
     params_other = lax.ppermute(params, "seq", SIBLING)
 
     half = shape((16, 272, 128), BF)
     slots = shape((count, 256), F32)
     small = shape((16, 24, 128), BF)
     row = shape((8, 128), F32)
-    own, other, logits, combine = call(
-        route_kernel, (half, half, slots, slots), params, params_other, z
+    own, other, logits, combine, params = call(
+        route_kernel,
+        (half, half, slots, slots, shape((256, 2048), BF)),
+        at,
+        params,
+        params_other,
+        z,
+        g,
     )
     sibling = lax.ppermute(other, "seq", SIBLING)
     pay = call(merge_core_kernel, half, own, sibling)
@@ -363,7 +406,6 @@
     own = swap(pay, "seq", CHIPS)
     other = lax.ppermute(own, "seq", SIBLING)
     part = shape((16, 144, 128), BF)
-    by_feature = shape((16, count, 128), BF)
     mixed, own, other, guess, dispatch, dispatch_cot, term, ins = call(
         mix_kernel,
         (
@@ -373,6 +415,7 @@
         own,
         other,
         z,
+        g,
         logits,
         combine,
     )
@@ -383,24 +426,28 @@
     pay = swap(pay, "expert")
     mixed = pay[:, 0:count].reshape(tokens.shape)
     param_grad, column = call(
-        param_expert_kernel, (shape((32, 8, 128), F32), row), expert_at, pay, guess, slot_piece
-    )
-    token_grad = call(
+        param_expert_kernel, (shape((1, 8, 128), F32), row), at, pay, guess, slot_piece
+    )
+    token_grad, param_grad = call(
         token_kernel,
-        by_feature,
+        (by_feature, shape((1, 8, 128), F32)),
         column,
         lax.ppermute(column, "seq", SIBLING),
         params,
-        params_other,
         dispatch,
         dispatch_cot,
         term,
         ins,
+        param_grad,
     )
     token_grad = swap(token_grad, "expert").reshape(tokens.shape)
-    param_grad = swap(param_grad, "seq")
-    param_grad = (
-        param_grad.reshape(16, 2, 8, 128).transpose(1, 2, 0, 3).reshape(16, 2048).astype(BF)
+    param_grad = gather_chips(param_grad)
+    param_grad = call(
+        param_out_kernel,
+        shape((16, 2048), BF),
+        at,
+        param_grad,
+        lax.ppermute(param_grad, "seq", SIBLING),
     )
     return (mixed, token_grad, param_grad, w_in_grad[None], w_out_grad[None])
 

time: 267 us -> 285 us (1.067)
  the two profiles are of different devices: /device:TPU:32 before, /device:TPU:1 now
where the time goes in v2:
time: 285 us; the launch traced here: 284 us
  blocking collectives  163 us (57%)
  starting transfers between devices  77.6 us (27%)
  waiting for transfers between devices  27.5 us (10%)
  Pallas kernels  9.93 us (3%)
    all_to_all x9, blocking collectives, swap(): lax.all_to_all(array, axis, split_axis=0, concat_axis=0, tiled=True, axis...  163 us
    ppermute x8, starting transfers between devices, gather_chips(): block = jnp.concatenate([block, lax.ppermute(block, 'seq', pairs)], axis=0)  24 us
    ppermute x8, waiting for transfers between devices, gather_chips(): block = jnp.concatenate([block, lax.ppermute(block, 'seq', pairs)], axis=0)  19.7 us
    all_to_all x2, starting transfers between devices, swap(): lax.all_to_all(array, axis, split_axis=0, concat_axis=0, tiled=True, axis...  17.1 us
    ppermute x1, starting transfers between devices, local(): lax.ppermute(column, 'seq', SIBLING)  10.1 us
    pallas_call x14, Pallas kernels, call(): pl.pallas_call(body, out_shape=out_shape, in_specs=[smem if arg.dtype ==...  9.93 us
    ppermute x1, starting transfers between devices, local(): params_other = lax.ppermute(params, 'seq', SIBLING)  6.34 us
    ppermute x1, starting transfers between devices, local(): lax.ppermute(param_grad, 'seq', SIBLING)  6.2 us
  transfers between devices with their start and end apart: 16, of which 11 were waited for; matrix products, arithmetic and copies ran while one was open for 1% of the time, Pallas kernels for 0%

profile of v2, /device:TPU:1, one launch (start us, length us, event | category | flops | bytes accessed | tf_op | source)
XLA Modules:
  0.0 284.2 jit_solution(12851935738218584636)
XLA Ops:
  2.4 29.3 %all_to_all.55.z_ref = bf16[16,72,128]{2,1,0:T(8,128)(2,1)S(1)} all-to-all(bf16[16,72,128]{2,1,0:T(8,128)(2,1)S(1)} %pad_maximum_fusion), channel_id=1, replica_groups=mesh['seq'=32,'expert'=16] {'expert'}, dimensions={0} | all-to-all | bytes 589824 | tf_op jit(solution)/shard_map/all_to_all | solution.py:343
  32.4 3.2 %collective-permute-start = (bf16[1,128,128]{2,1,0:T(8,128)(2,1)S(1)}, bf16[1,128,128]{2,1,0:T(8,128)(2,1)S(1)}, u32[]{:S(2)}, u32[]{:S(2)}) collective-permute-start(bf16[1,128,128]{2,1,0:T(8,128)(2,1)S(1)} %get-tuple-element.32), channel_id=1, source_target_pairs={{0,32},{16,48},{32,0},{48,16},{64,96},{80,112},{96,64},{112,80},{1... | collective-permute-start | bytes 98312 | tf_op jit(solution)/shard_map/ppermute | solution.py:338
  37.4 4.6 %collective-permute-start.1 = (bf16[2,128,128]{2,1,0:T(8,128)(2,1)S(1)}, bf16[2,128,128]{2,1,0:T(8,128)(2,1)S(1)}, u32[]{:S(2)}, u32[]{:S(2)}) collective-permute-start(bf16[2,128,128]{2,1,0:T(8,128)(2,1)S(1)} %pad_maximum_fusion.3), channel_id=1, source_target_pairs={{0,96},{16,112},{32,64},{48,80},{64,32},{80,48},{96,0},{112,16},{1... | collective-permute-start | bytes 196616 | tf_op jit(solution)/shard_map/ppermute | solution.py:338
  43.7 3.1 %collective-permute-start.2 = (bf16[4,128,128]{2,1,0:T(8,128)(2,1)S(1)}, bf16[4,128,128]{2,1,0:T(8,128)(2,1)S(1)}, u32[]{:S(2)}, u32[]{:S(2)}) collective-permute-start(bf16[4,128,128]{2,1,0:T(8,128)(2,1)S(1)} %pad_maximum_fusion.2), channel_id=1, source_target_pairs={{0,128},{16,144},{32,160},{48,176},{64,192},{80,208},{96,224},{112... | collective-permute-start | bytes 393224 | tf_op jit(solution)/shard_map/ppermute | solution.py:338
  46.8 11.4 %all-to-all-start.1 = ((bf16[16,64,128]{2,1,0:T(8,128)(2,1)}), bf16[16,64,128]{2,1,0:T(8,128)(2,1)S(1)}, u32[]{:S(2)}, u32[]{:S(2)}) async-start(bf16[16,64,128]{2,1,0:T(8,128)(2,1)} %get-tuple-element.33), calls=%async_computation.1 | async-start | bytes 524288 | tf_op jit(solution)/shard_map/all_to_all | solution.py:343
  58.3 3.7 %collective-permute-start.3 = (bf16[8,128,128]{2,1,0:T(8,128)(2,1)S(1)}, bf16[8,128,128]{2,1,0:T(8,128)(2,1)S(1)}, u32[]{:S(2)}, u32[]{:S(2)}) collective-permute-start(bf16[8,128,128]{2,1,0:T(8,128)(2,1)S(1)} %pad_maximum_fusion.1), channel_id=1, source_target_pairs={{0,384},{16,400},{32,416},{48,432},{64,448},{80,464},{96,480},{112... | collective-permute-start | bytes 786440 | tf_op jit(solution)/shard_map/ppermute | solution.py:338
  62.1 4.8 %collective-permute-done.3 = bf16[8,128,128]{2,1,0:T(8,128)(2,1)S(1)} collective-permute-done((bf16[8,128,128]{2,1,0:T(8,128)(2,1)S(1)}, bf16[8,128,128]{2,1,0:T(8,128)(2,1)S(1)}, u32[]{:S(2)}, u32[]{:S(2)}) %collective-permute-start.3) | collective-permute-done | bytes 262176 | tf_op jit(solution)/shard_map/ppermute | solution.py:338
  66.9 6.3 %collective-permute-start.4 = (bf16[16,128,128]{2,1,0:T(8,128)(2,1)S(1)}, bf16[16,128,128]{2,1,0:T(8,128)(2,1)S(1)}, u32[]{:S(2)}, u32[]{:S(2)}) collective-permute-start(bf16[16,128,128]{2,1,0:T(8,128)(2,1)S(1)} %constant_dynamic-update-slice_fusion.pown_ref), channel_id=1, source_target_pairs={{0,16},{16,0},{32,48},{48,32},{64,80},{80,64},{96,112},{112,96},{1... | collective-permute-start | bytes 1572872 | tf_op jit(solution)/shard_map/ppermute | solution.py:368
  74.8 2.2 shard_map.93
  77.1 5.5 %collective-permute-start.5 = (bf16[16,272,128]{2,1,0:T(8,128)(2,1)S(1)}, bf16[16,272,128]{2,1,0:T(8,128)(2,1)S(1)}, u32[]{:S(2)}, u32[]{:S(2)}) collective-permute-start(bf16[16,272,128]{2,1,0:T(8,128)(2,1)S(1)} %get-tuple-element.35), channel_id=1, source_target_pairs={{0,16},{16,0},{32,48},{48,32},{64,80},{80,64},{96,112},{112,96},{1... | collective-permute-start | bytes 3342344 | tf_op jit(solution)/shard_map/ppermute | solution.py:383
  82.5 2.4 collective-permute-done.5.sib_ref
  85.4 23.2 %all_to_all.56.r_ref = bf16[16,272,128]{2,1,0:T(8,128)(2,1)S(1)} all-to-all(bf16[16,272,128]{2,1,0:T(8,128)(2,1)S(1)} %shard_map.94), channel_id=1, replica_groups={{0,32,64,96,128,160,192,224,256,288,320,352,384,416,448,480},{16,48,80,..., dimensions={0} | all-to-all | bytes 2228224 | tf_op jit(solution)/shard_map/all_to_all | solution.py:343
  109.1 19.6 %all_to_all.57.r_ref = bf16[16,24,128]{2,1,0:T(8,128)(2,1)S(1)} all-to-all(bf16[16,24,128]{2,1,0:T(8,128)(2,1)S(1)} %shard_map.95), channel_id=1, replica_groups=mesh['seq'=32,'expert'=16] {'expert'}, dimensions={0} | all-to-all | bytes 196608 | tf_op jit(solution)/shard_map/all_to_all | solution.py:343
  129.0 14.2 %all_to_all.58.r_ref = bf16[32,16,128]{2,1,0:T(8,128)(2,1)S(1)} all-to-all(bf16[32,16,128]{2,1,0:T(8,128)(2,1)S(1)} %get-tuple-element.36), channel_id=1, replica_groups=mesh['seq'=32,'expert'=16] {'seq'}, dimensions={0} | all-to-all | bytes 262144 | tf_op jit(solution)/shard_map/all_to_all | solution.py:343
  143.9 11.3 %all_to_all.59.r_ref = bf16[32,16,128]{2,1,0:T(8,128)(2,1)S(1)} all-to-all(bf16[32,16,128]{2,1,0:T(8,128)(2,1)S(1)} %get-tuple-element.37), channel_id=1, replica_groups=mesh['seq'=32,'expert'=16] {'seq'}, dimensions={0} | all-to-all | bytes 262144 | tf_op jit(solution)/shard_map/all_to_all | solution.py:343
  155.3 14.7 %all_to_all.60.r_ref = bf16[16,24,128]{2,1,0:T(8,128)(2,1)S(1)} all-to-all(bf16[16,24,128]{2,1,0:T(8,128)(2,1)S(1)} %shard_map.98), channel_id=1, replica_groups=mesh['seq'=32,'expert'=16] {'expert'}, dimensions={0} | all-to-all | bytes 196608 | tf_op jit(solution)/shard_map/all_to_all | solution.py:343
  170.2 17.3 %all_to_all.61.own_ref = bf16[16,272,128]{2,1,0:T(8,128)(2,1)S(1)} all-to-all(bf16[16,272,128]{2,1,0:T(8,128)(2,1)S(1)} %shard_map.99), channel_id=1, replica_groups={{0,32,64,96,128,160,192,224,256,288,320,352,384,416,448,480},{16,48,80,..., dimensions={0} | all-to-all | bytes 2228224 | tf_op jit(solution)/shard_map/all_to_all | solution.py:343
  187.5 6.1 %collective-permute-start.6 = (bf16[16,272,128]{2,1,0:T(8,128)(2,1)S(1)}, bf16[16,272,128]{2,1,0:T(8,128)(2,1)S(1)}, u32[]{:S(2)}, u32[]{:S(2)}) collective-permute-start(bf16[16,272,128]{2,1,0:T(8,128)(2,1)S(1)} %all_to_all.61.own_ref), channel_id=1, source_target_pairs={{0,16},{16,0},{32,48},{48,32},{64,80},{80,64},{96,112},{112,96},{1... | collective-permute-start | bytes 3342344 | tf_op jit(solution)/shard_map/ppermute | solution.py:407
  193.6 2.4 collective-permute-done.6.other_ref
  197.4 2.3 collective-permute-start.7
  201.4 14.4 %all_to_all.62.r_ref = bf16[16,144,128]{2,1,0:T(8,128)(2,1)S(1)} all-to-all(bf16[16,144,128]{2,1,0:T(8,128)(2,1)S(1)} %shard_map.101), channel_id=1, replica_groups={{0,32,64,96,128,160,192,224,256,288,320,352,384,416,448,480},{16,48,80,..., dimensions={0} | all-to-all | bytes 1179648 | tf_op jit(solution)/shard_map/all_to_all | solution.py:343
  216.0 18.6 %all_to_all.63.r_ref = bf16[16,80,128]{2,1,0:T(8,128)(2,1)S(1)} all-to-all(bf16[16,80,128]{2,1,0:T(8,128)(2,1)S(1)} %shard_map.102), channel_id=1, replica_groups=mesh['seq'=32,'expert'=16] {'expert'}, dimensions={0} | all-to-all | bytes 655360 | tf_op jit(solution)/shard_map/all_to_all | solution.py:343
  235.2 10.1 %collective-permute-start.8 = (f32[8,128]{1,0:T(8,128)S(1)}, f32[8,128]{1,0:T(8,128)S(1)}, u32[]{:S(2)}, u32[]{:S(2)}) collective-permute-start(f32[8,128]{1,0:T(8,128)S(1)} %get-tuple-element.46.colown_ref), channel_id=1, source_target_pairs={{0,16},{16,0},{32,48},{48,32},{64,80},{80,64},{96,112},{112,96},{1... | collective-permute-start | bytes 12296 | tf_op jit(solution)/shard_map/ppermute | solution.py:435
  247.6 5.7 %all-to-all-start.10 = ((bf16[16,64,128]{2,1,0:T(8,128)(2,1)}), bf16[16,64,128]{2,1,0:T(8,128)(2,1)S(1)}, u32[]{:S(2)}, u32[]{:S(2)}) async-start(bf16[16,64,128]{2,1,0:T(8,128)(2,1)} %get-tuple-element.53), calls=%async_computation.10 | async-start | bytes 524288 | tf_op jit(solution)/shard_map/all_to_all | solution.py:343
  253.3 2.2 collective-permute-start.9
  255.5 2.2 collective-permute-done.9
  257.7 2.6 collective-permute-start.10
  260.3 3.3 %collective-permute-done.10 = f32[2,8,128]{2,1,0:T(8,128)S(1)} collective-permute-done((f32[2,8,128]{2,1,0:T(8,128)S(1)}, f32[2,8,128]{2,1,0:T(8,128)S(1)}, u32[]{:S(2)}, u32[]{:S(2)}) %collective-permute-start.10) | collective-permute-done | bytes 8224 | tf_op jit(solution)/shard_map/ppermute | solution.py:338
  265.5 2.8 collective-permute-done.11
  268.4 2.6 collective-permute-start.12
  271.0 3.2 %collective-permute-done.12 = f32[8,8,128]{2,1,0:T(8,128)S(1)} collective-permute-done((f32[8,8,128]{2,1,0:T(8,128)S(1)}, f32[8,8,128]{2,1,0:T(8,128)S(1)}, u32[]{:S(2)}, u32[]{:S(2)}) %collective-permute-start.12) | collective-permute-done | bytes 32800 | tf_op jit(solution)/shard_map/ppermute | solution.py:338
  274.2 6.2 %collective-permute-start.13 = (f32[16,8,128]{2,1,0:T(8,128)S(1)}, f32[16,8,128]{2,1,0:T(8,128)S(1)}, u32[]{:S(2)}, u32[]{:S(2)}) collective-permute-start(f32[16,8,128]{2,1,0:T(8,128)S(1)} %constant_dynamic-update-slice_fusion.5.own_ref), channel_id=1, source_target_pairs={{0,16},{16,0},{32,48},{48,32},{64,80},{80,64},{96,112},{112,96},{1... | collective-permute-start | bytes 196616 | tf_op jit(solution)/shard_map/ppermute | solution.py:450
  (53 shorter events, 21.6 us)
Async XLA Ops:
  0.6 31.1 %copy-start.2 = (bf16[1,1024,128]{2,1,0:T(8,128)(2,1)S(1)}, bf16[1,1024,128]{2,1,0:T(8,128)(2,1)}, u32[]{:S(2)}) copy-start(bf16[1,1024,128]{2,1,0:T(8,128)(2,1)} %param.9) | copy-start | bytes 786436
  32.4 4.9 %collective-permute-start = (bf16[1,128,128]{2,1,0:T(8,128)(2,1)S(1)}, bf16[1,128,128]{2,1,0:T(8,128)(2,1)S(1)}, u32[]{:S(2)}, u32[]{:S(2)}) collective-permute-start(bf16[1,128,128]{2,1,0:T(8,128)(2,1)S(1)} %get-tuple-element.32), channel_id=1, source_target_pairs={{0,32},{16,48},{32,0},{48,16},{64,96},{80,112},{96,64},{112,80},{1... | collective-permute-start | bytes 98312 | tf_op jit(solution)/shard_map/ppermute | solution.py:338
  37.4 6.3 %collective-permute-start.1 = (bf16[2,128,128]{2,1,0:T(8,128)(2,1)S(1)}, bf16[2,128,128]{2,1,0:T(8,128)(2,1)S(1)}, u32[]{:S(2)}, u32[]{:S(2)}) collective-permute-start(bf16[2,128,128]{2,1,0:T(8,128)(2,1)S(1)} %pad_maximum_fusion.3), channel_id=1, source_target_pairs={{0,96},{16,112},{32,64},{48,80},{64,32},{80,48},{96,0},{112,16},{1... | collective-permute-start | bytes 196616 | tf_op jit(solution)/shard_map/ppermute | solution.py:338
  43.7 14.6 %collective-permute-start.2 = (bf16[4,128,128]{2,1,0:T(8,128)(2,1)S(1)}, bf16[4,128,128]{2,1,0:T(8,128)(2,1)S(1)}, u32[]{:S(2)}, u32[]{:S(2)}) collective-permute-start(bf16[4,128,128]{2,1,0:T(8,128)(2,1)S(1)} %pad_maximum_fusion.2), channel_id=1, source_target_pairs={{0,128},{16,144},{32,160},{48,176},{64,192},{80,208},{96,224},{112... | collective-permute-start | bytes 393224 | tf_op jit(solution)/shard_map/ppermute | solution.py:338
  46.8 26.6 %all-to-all-start.1 = ((bf16[16,64,128]{2,1,0:T(8,128)(2,1)}), bf16[16,64,128]{2,1,0:T(8,128)(2,1)S(1)}, u32[]{:S(2)}, u32[]{:S(2)}) async-start(bf16[16,64,128]{2,1,0:T(8,128)(2,1)} %get-tuple-element.33), calls=%async_computation.1 | async-start | bytes 524288 | tf_op jit(solution)/shard_map/all_to_all | solution.py:343
  58.3 8.6 %collective-permute-start.3 = (bf16[8,128,128]{2,1,0:T(8,128)(2,1)S(1)}, bf16[8,128,128]{2,1,0:T(8,128)(2,1)S(1)}, u32[]{:S(2)}, u32[]{:S(2)}) collective-permute-start(bf16[8,128,128]{2,1,0:T(8,128)(2,1)S(1)} %pad_maximum_fusion.1), channel_id=1, source_target_pairs={{0,384},{16,400},{32,416},{48,432},{64,448},{80,464},{96,480},{112... | collective-permute-start | bytes 786440 | tf_op jit(solution)/shard_map/ppermute | solution.py:338
  66.9 7.9 %collective-permute-start.4 = (bf16[16,128,128]{2,1,0:T(8,128)(2,1)S(1)}, bf16[16,128,128]{2,1,0:T(8,128)(2,1)S(1)}, u32[]{:S(2)}, u32[]{:S(2)}) collective-permute-start(bf16[16,128,128]{2,1,0:T(8,128)(2,1)S(1)} %constant_dynamic-update-slice_fusion.pown_ref), channel_id=1, source_target_pairs={{0,16},{16,0},{32,48},{48,32},{64,80},{80,64},{96,112},{112,96},{1... | collective-permute-start | bytes 1572872 | tf_op jit(solution)/shard_map/ppermute | solution.py:368
  77.1 7.8 %collective-permute-start.5 = (bf16[16,272,128]{2,1,0:T(8,128)(2,1)S(1)}, bf16[16,272,128]{2,1,0:T(8,128)(2,1)S(1)}, u32[]{:S(2)}, u32[]{:S(2)}) collective-permute-start(bf16[16,272,128]{2,1,0:T(8,128)(2,1)S(1)} %get-tuple-element.35), channel_id=1, source_target_pairs={{0,16},{16,0},{32,48},{48,32},{64,80},{80,64},{96,112},{112,96},{1... | collective-permute-start | bytes 3342344 | tf_op jit(solution)/shard_map/ppermute | solution.py:383
  108.6 34.6 %copy-start = (bf16[1,2048,128]{2,1,0:T(8,128)(2,1)S(1)}, bf16[1,2048,128]{2,1,0:T(8,128)(2,1)}, u32[]{:S(2)}) copy-start(bf16[1,2048,128]{2,1,0:T(8,128)(2,1)} %param.7) | copy-start | bytes 1572868
  108.6 34.6 %copy-start.1 = (bf16[1,128,2048]{2,1,0:T(8,128)(2,1)S(1)}, bf16[1,128,2048]{2,1,0:T(8,128)(2,1)}, u32[]{:S(2)}) copy-start(bf16[1,128,2048]{2,1,0:T(8,128)(2,1)} %param.8) | copy-start | bytes 1572868
  187.5 8.4 %collective-permute-start.6 = (bf16[16,272,128]{2,1,0:T(8,128)(2,1)S(1)}, bf16[16,272,128]{2,1,0:T(8,128)(2,1)S(1)}, u32[]{:S(2)}, u32[]{:S(2)}) collective-permute-start(bf16[16,272,128]{2,1,0:T(8,128)(2,1)S(1)} %all_to_all.61.own_ref), channel_id=1, source_target_pairs={{0,16},{16,0},{32,48},{48,32},{64,80},{80,64},{96,112},{112,96},{1... | collective-permute-start | bytes 3342344 | tf_op jit(solution)/shard_map/ppermute | solution.py:407
  197.4 3.9 %collective-permute-start.7 = (bf16[16,144,128]{2,1,0:T(8,128)(2,1)S(1)}, bf16[16,144,128]{2,1,0:T(8,128)(2,1)S(1)}, u32[]{:S(2)}, u32[]{:S(2)}) collective-permute-start(bf16[16,144,128]{2,1,0:T(8,128)(2,1)S(1)} %get-tuple-element.43), channel_id=1, source_target_pairs={{0,16},{16,0},{32,48},{48,32},{64,80},{80,64},{96,112},{112,96},{1... | collective-permute-start | bytes 1769480 | tf_op jit(solution)/shard_map/ppermute | solution.py:422
  235.2 11.3 %collective-permute-start.8 = (f32[8,128]{1,0:T(8,128)S(1)}, f32[8,128]{1,0:T(8,128)S(1)}, u32[]{:S(2)}, u32[]{:S(2)}) collective-permute-start(f32[8,128]{1,0:T(8,128)S(1)} %get-tuple-element.46.colown_ref), channel_id=1, source_target_pairs={{0,16},{16,0},{32,48},{48,32},{64,80},{80,64},{96,112},{112,96},{1... | collective-permute-start | bytes 12296 | tf_op jit(solution)/shard_map/ppermute | solution.py:435
  247.6 35.8 %all-to-all-start.10 = ((bf16[16,64,128]{2,1,0:T(8,128)(2,1)}), bf16[16,64,128]{2,1,0:T(8,128)(2,1)S(1)}, u32[]{:S(2)}, u32[]{:S(2)}) async-start(bf16[16,64,128]{2,1,0:T(8,128)(2,1)} %get-tuple-element.53), calls=%async_computation.10 | async-start | bytes 524288 | tf_op jit(solution)/shard_map/all_to_all | solution.py:343
  253.3 4.4 %collective-permute-start.9 = (f32[1,8,128]{2,1,0:T(8,128)S(1)}, f32[1,8,128]{2,1,0:T(8,128)S(1)}, u32[]{:S(2)}, u32[]{:S(2)}) collective-permute-start(f32[1,8,128]{2,1,0:T(8,128)S(1)} %get-tuple-element.54), channel_id=1, source_target_pairs={{0,32},{16,48},{32,0},{48,16},{64,96},{80,112},{96,64},{112,80},{1... | collective-permute-start | bytes 12296 | tf_op jit(solution)/shard_map/ppermute | solution.py:338
  257.7 5.9 %collective-permute-start.10 = (f32[2,8,128]{2,1,0:T(8,128)S(1)}, f32[2,8,128]{2,1,0:T(8,128)S(1)}, u32[]{:S(2)}, u32[]{:S(2)}) collective-permute-start(f32[2,8,128]{2,1,0:T(8,128)S(1)} %pad_maximum_fusion.6), channel_id=1, source_target_pairs={{0,96},{16,112},{32,64},{48,80},{64,32},{80,48},{96,0},{112,16},{1... | collective-permute-start | bytes 24584 | tf_op jit(solution)/shard_map/ppermute | solution.py:338
  263.6 4.8 %collective-permute-start.11 = (f32[4,8,128]{2,1,0:T(8,128)S(1)}, f32[4,8,128]{2,1,0:T(8,128)S(1)}, u32[]{:S(2)}, u32[]{:S(2)}) collective-permute-start(f32[4,8,128]{2,1,0:T(8,128)S(1)} %pad_maximum_fusion.5), channel_id=1, source_target_pairs={{0,128},{16,144},{32,160},{48,176},{64,192},{80,208},{96,224},{112... | collective-permute-start | bytes 49160 | tf_op jit(solution)/shard_map/ppermute | solution.py:338
  268.4 5.9 %collective-permute-start.12 = (f32[8,8,128]{2,1,0:T(8,128)S(1)}, f32[8,8,128]{2,1,0:T(8,128)S(1)}, u32[]{:S(2)}, u32[]{:S(2)}) collective-permute-start(f32[8,8,128]{2,1,0:T(8,128)S(1)} %pad_maximum_fusion.4), channel_id=1, source_target_pairs={{0,384},{16,400},{32,416},{48,432},{64,448},{80,464},{96,480},{112... | collective-permute-start | bytes 98312 | tf_op jit(solution)/shard_map/ppermute | solution.py:338
  274.2 8.0 %collective-permute-start.13 = (f32[16,8,128]{2,1,0:T(8,128)S(1)}, f32[16,8,128]{2,1,0:T(8,128)S(1)}, u32[]{:S(2)}, u32[]{:S(2)}) collective-permute-start(f32[16,8,128]{2,1,0:T(8,128)S(1)} %constant_dynamic-update-slice_fusion.5.own_ref), channel_id=1, source_target_pairs={{0,16},{16,0},{32,48},{48,32},{64,80},{80,64},{96,112},{112,96},{1... | collective-permute-start | bytes 196616 | tf_op jit(solution)/shard_map/ppermute | solution.py:450

commit v3 on v1

--- a/solution.py
+++ b/solution.py
@@ -53,6 +53,17 @@
 def tokens_of(z_ref):
     count = (z_ref.shape[1] - 8) // 2
     return lanes(z_ref, slice(0, count)), lanes(z_ref, slice(count, 2 * count))
+
+
+def stage_kernel(at_ref, x_ref, g_ref, slot_ref, pay_ref):
+    count = x_ref.shape[1]
+    feats = pl.ds(pl.multiple_of(at_ref[1] * 128, 128), 128)
+    both = slot_ref[:, feats].astype(F32)
+    piece = jnp.where(at_ref[2] == 0, both[0:8], both[8:16]).astype(BF)
+    for e in range(16):
+        pay_ref[e, 0:count, :] = x_ref[e]
+        pay_ref[e, count : 2 * count, :] = g_ref[e]
+        pay_ref[e, 2 * count : 2 * count + 8, :] = piece
 
 
 def route_kernel(pown_ref, pother_ref, z_ref, own_ref, other_ref, logit_ref, comb_ref):
@@ -283,8 +294,8 @@
     missed = jnp.sum(
         jnp.where(lane == at_ref[0] * 8 + row, missed, 0.0), axis=1, keepdims=True
     )
-    param = total[0:8] - missed * slot_ref[...]
-    for i in range(32):
+    param = (total[0:8] - missed * slot_ref[...]).astype(BF)
+    for i in range(16):
         pay_ref[i] = param
 
 
@@ -300,6 +311,15 @@
         tok_ref[f] = token_grad[:, f * 128 : (f + 1) * 128]
 
 
+def param_out_kernel(at_ref, own_ref, other_ref, out_ref):
+    first = at_ref[2] == 0
+    for f in range(16):
+        own, other = own_ref[f].astype(F32), other_ref[f].astype(F32)
+        out_ref[:, f * 128 : (f + 1) * 128] = jnp.concatenate(
+            [jnp.where(first, own, other), jnp.where(first, other, own)], axis=0
+        ).astype(BF)
+
+
 CHIPS = [list(range(0, 32, 2)), list(range(1, 32, 2))]
 SIBLING = [(i, i ^ 1) for i in range(32)]
 
@@ -313,17 +333,15 @@
 def local(tokens, slot_params, w_in, w_out, out_grad):
     count = tokens.shape[1] // 16
     seq_at = lax.axis_index("seq")
-    expert_at = lax.axis_index("expert").astype(jnp.int32).reshape(1)
-    piece = lax.dynamic_slice(
-        slot_params, ((seq_at % 2) * 8, (seq_at // 2) * 128), (8, 128)
-    )
-    block = jnp.concatenate(
-        [
-            tokens.reshape(16, count, 128),
-            out_grad.reshape(16, count, 128),
-            jnp.broadcast_to(piece[None], (16, 8, 128)),
-        ],
-        axis=1,
+    at = jnp.stack([lax.axis_index("expert"), seq_at // 2, seq_at % 2]).astype(jnp.int32)
+    by_feature = shape((16, count, 128), BF)
+    block = call(
+        stage_kernel,
+        shape((16, 2 * count + 8, 128), BF),
+        at,
+        tokens.reshape(by_feature.shape),
+        out_grad.reshape(by_feature.shape),
+        slot_params,
     )
     z = swap(block, "expert")
     mine = z[:, 2 * count :].reshape(128, 128)
@@ -363,7 +381,6 @@
     own = swap(pay, "seq", CHIPS)
     other = lax.ppermute(own, "seq", SIBLING)
     part = shape((16, 144, 128), BF)
-    by_feature = shape((16, count, 128), BF)
     mixed, own, other, guess, dispatch, dispatch_cot, term, ins = call(
         mix_kernel,
         (
@@ -383,7 +400,7 @@
     pay = swap(pay, "expert")
     mixed = pay[:, 0:count].reshape(tokens.shape)
     param_grad, column = call(
-        param_expert_kernel, (shape((32, 8, 128), F32), row), expert_at, pay, guess, slot_piece
+        param_expert_kernel, (shape((16, 8, 128), BF), row), at, pay, guess, slot_piece
     )
     token_grad = call(
         token_kernel,
@@ -398,9 +415,13 @@
         ins,
     )
     token_grad = swap(token_grad, "expert").reshape(tokens.shape)
-    param_grad = swap(param_grad, "seq")
-    param_grad = (
-        param_grad.reshape(16, 2, 8, 128).transpose(1, 2, 0, 3).reshape(16, 2048).astype(BF)
+    param_grad = swap(param_grad, "seq", CHIPS)
+    param_grad = call(
+        param_out_kernel,
+        shape((16, 2048), BF),
+        at,
+        param_grad,
+        lax.ppermute(param_grad, "seq", SIBLING),
     )
     return (mixed, token_grad, param_grad, w_in_grad[None], w_out_grad[None])
 

time: 267 us -> 267 us (level)
  blocking collectives: 178 us -> 204 us
  waiting for transfers between devices: 47.8 us -> 24.8 us
  starting transfers between devices: 25.7 us -> 21.3 us
    all_to_all x9 -> x10, blocking collectives: 178 us -> 204 us  [swap(): lax.all_to_all(array, axis, split_axis=0, concat_axis=0, tiled=True, axis...]
    all_to_all x3 -> x2, waiting for transfers between devices: 37.9 us -> 14.6 us  [swap(): lax.all_to_all(array, axis, split_axis=0, concat_axis=0, tiled=True, axis...]
    all_to_all x3 -> x2, starting transfers between devices: 15.6 us -> 9.58 us  [swap(): lax.all_to_all(array, axis, split_axis=0, concat_axis=0, tiled=True, axis...]
    unnamed x5 -> x11, local copies, waits for them, and re-layouts: 0.71 us -> 3.45 us
    pallas_call x12 -> x14, Pallas kernels: 7.22 us -> 9.4 us  [call(): pl.pallas_call(body, out_shape=out_shape, in_specs=[smem if arg.dtype ==...]
  transfers between devices with their start and end apart: 8 -> 8, of which waited for: 8 -> 7; matrix products, arithmetic and copies ran while one was open for 1% -> 1% of each run, Pallas kernels for 0% -> 1%
where the time goes in v3:
time: 267 us
  blocking collectives  204 us (76%)
  waiting for transfers between devices  24.8 us (9%)
  starting transfers between devices  21.3 us (8%)
  Pallas kernels  9.4 us (4%)
  local copies, waits for them, and re-layouts  4.28 us (2%)
    all_to_all x10, blocking collectives, swap(): lax.all_to_all(array, axis, split_axis=0, concat_axis=0, tiled=True, axis...  204 us
    all_to_all x2, waiting for transfers between devices, swap(): lax.all_to_all(array, axis, split_axis=0, concat_axis=0, tiled=True, axis...  14.6 us
    all_to_all x2, starting transfers between devices, swap(): lax.all_to_all(array, axis, split_axis=0, concat_axis=0, tiled=True, axis...  9.58 us
    pallas_call x14, Pallas kernels, call(): pl.pallas_call(body, out_shape=out_shape, in_specs=[smem if arg.dtype ==...  9.4 us
  transfers between devices with their start and end apart: 8, of which 7 were waited for; matrix products, arithmetic and copies ran while one was open for 1% of the time, Pallas kernels for 1%

profile of v3, /device:TPU:32, one launch (start us, length us, event | category | flops | bytes accessed | tf_op | source)
XLA Modules:
  0.0 266.6 jit_solution(11755750280268240647)
XLA Ops:
  4.1 48.1 %all_to_all.60.z_ref = bf16[16,136,128]{2,1,0:T(8,128)(2,1)S(1)} all-to-all(bf16[16,136,128]{2,1,0:T(8,128)(2,1)S(1)} %shard_map.92), channel_id=1, replica_groups=mesh['seq'=32,'expert'=16] {'expert'}, dimensions={0} | all-to-all | bytes 1114112 | tf_op jit(solution)/shard_map/all_to_all | solution.py:328
  52.2 17.2 %all_to_all.61.pown_ref = bf16[16,128,128]{2,1,0:T(8,128)(2,1)S(1)} all-to-all(bf16[16,128,128]{2,1,0:T(8,128)(2,1)S(1)} %broadcast_in_dim.14), channel_id=1, replica_groups={{0,32,64,96,128,160,192,224,256,288,320,352,384,416,448,480},{16,48,80,..., dimensions={0} | all-to-all | bytes 1048576 | tf_op jit(solution)/shard_map/all_to_all | solution.py:328
  69.5 1.9 collective-permute-start
  71.4 1.9 collective-permute-done.pother_ref
  73.2 1.3 shard_map.93
  74.6 2.0 collective-permute-start.1
  76.6 2.6 collective-permute-done.1.sib_ref
  79.7 21.4 %all_to_all.62.r_ref = bf16[16,272,128]{2,1,0:T(8,128)(2,1)S(1)} all-to-all(bf16[16,272,128]{2,1,0:T(8,128)(2,1)S(1)} %shard_map.94), channel_id=1, replica_groups={{0,32,64,96,128,160,192,224,256,288,320,352,384,416,448,480},{16,48,80,..., dimensions={0} | all-to-all | bytes 2228224 | tf_op jit(solution)/shard_map/all_to_all | solution.py:328
  101.6 16.7 %all_to_all.63.r_ref = bf16[16,24,128]{2,1,0:T(8,128)(2,1)S(1)} all-to-all(bf16[16,24,128]{2,1,0:T(8,128)(2,1)S(1)} %shard_map.95), channel_id=1, replica_groups=mesh['seq'=32,'expert'=16] {'expert'}, dimensions={0} | all-to-all | bytes 196608 | tf_op jit(solution)/shard_map/all_to_all | solution.py:328
  118.6 11.4 %all_to_all.64.r_ref = bf16[32,16,128]{2,1,0:T(8,128)(2,1)S(1)} all-to-all(bf16[32,16,128]{2,1,0:T(8,128)(2,1)S(1)} %get-tuple-element.29), channel_id=1, replica_groups=mesh['seq'=32,'expert'=16] {'seq'}, dimensions={0} | all-to-all | bytes 262144 | tf_op jit(solution)/shard_map/all_to_all | solution.py:328
  130.8 11.3 %all_to_all.65.r_ref = bf16[32,16,128]{2,1,0:T(8,128)(2,1)S(1)} all-to-all(bf16[32,16,128]{2,1,0:T(8,128)(2,1)S(1)} %get-tuple-element.30), channel_id=1, replica_groups=mesh['seq'=32,'expert'=16] {'seq'}, dimensions={0} | all-to-all | bytes 262144 | tf_op jit(solution)/shard_map/all_to_all | solution.py:328
  142.2 17.2 %all_to_all.66.r_ref = bf16[16,24,128]{2,1,0:T(8,128)(2,1)S(1)} all-to-all(bf16[16,24,128]{2,1,0:T(8,128)(2,1)S(1)} %shard_map.98), channel_id=1, replica_groups=mesh['seq'=32,'expert'=16] {'expert'}, dimensions={0} | all-to-all | bytes 196608 | tf_op jit(solution)/shard_map/all_to_all | solution.py:328
  159.6 19.1 %all_to_all.67.own_ref = bf16[16,272,128]{2,1,0:T(8,128)(2,1)S(1)} all-to-all(bf16[16,272,128]{2,1,0:T(8,128)(2,1)S(1)} %shard_map.99), channel_id=1, replica_groups={{0,32,64,96,128,160,192,224,256,288,320,352,384,416,448,480},{16,48,80,..., dimensions={0} | all-to-all | bytes 2228224 | tf_op jit(solution)/shard_map/all_to_all | solution.py:328
  178.7 1.9 collective-permute-start.2
  180.6 2.7 %collective-permute-done.2.other_ref = bf16[16,272,128]{2,1,0:T(8,128)(2,1)S(1)} collective-permute-done((bf16[16,272,128]{2,1,0:T(8,128)(2,1)S(1)}, bf16[16,272,128]{2,1,0:T(8,128)(2,1)S(1)}, u32[]{:S(2)}, u32[]{:S(2)}) %collective-permute-start.2) | collective-permute-done | bytes 1114144 | tf_op jit(solution)/shard_map/ppermute | solution.py:382
  183.3 1.4 shard_map.100
  184.8 2.0 collective-permute-start.3
  186.8 1.8 collective-permute-done.3.sib_ref
  188.8 15.8 %all_to_all.68.r_ref = bf16[16,144,128]{2,1,0:T(8,128)(2,1)S(1)} all-to-all(bf16[16,144,128]{2,1,0:T(8,128)(2,1)S(1)} %shard_map.101), channel_id=1, replica_groups={{0,32,64,96,128,160,192,224,256,288,320,352,384,416,448,480},{16,48,80,..., dimensions={0} | all-to-all | bytes 1179648 | tf_op jit(solution)/shard_map/all_to_all | solution.py:328
  204.7 25.4 %all_to_all.69.r_ref = bf16[16,80,128]{2,1,0:T(8,128)(2,1)S(1)} all-to-all(bf16[16,80,128]{2,1,0:T(8,128)(2,1)S(1)} %shard_map.102), channel_id=1, replica_groups=mesh['seq'=32,'expert'=16] {'expert'}, dimensions={0} | all-to-all | bytes 655360 | tf_op jit(solution)/shard_map/all_to_all | solution.py:328
  230.1 1.3 shard_map.103
  231.4 3.9 %all-to-all-start.11 = ((bf16[16,8,128]{2,1,0:T(8,128)(2,1)}), bf16[16,8,128]{2,1,0:T(8,128)(2,1)S(1)}, u32[]{:S(2)}, u32[]{:S(2)}) async-start(bf16[16,8,128]{2,1,0:T(8,128)(2,1)} %get-tuple-element.44), calls=%async_computation.11 | async-start | bytes 65536 | tf_op jit(solution)/shard_map/all_to_all | solution.py:328
  235.3 1.9 collective-permute-start.4
  237.2 1.1 collective-permute-done.4.colother_ref
  238.4 1.2 shard_map.104
  239.5 3.4 %all-to-all-done.11.own_ref = bf16[16,8,128]{2,1,0:T(8,128)(2,1)S(1)} async-done(((bf16[16,8,128]{2,1,0:T(8,128)(2,1)}), bf16[16,8,128]{2,1,0:T(8,128)(2,1)S(1)}, u32[]{:S(2)}, u32[]{:S(2)}) %all-to-all-start.11) | async-done | bytes 32800 | tf_op jit(solution)/shard_map/all_to_all | solution.py:328
  242.9 5.7 %all-to-all-start.10 = ((bf16[16,64,128]{2,1,0:T(8,128)(2,1)}), bf16[16,64,128]{2,1,0:T(8,128)(2,1)S(1)}, u32[]{:S(2)}, u32[]{:S(2)}) async-start(bf16[16,64,128]{2,1,0:T(8,128)(2,1)} %shard_map.104), calls=%async_computation.10 | async-start | bytes 524288 | tf_op jit(solution)/shard_map/all_to_all | solution.py:328
  248.6 1.1 fusion
  249.7 1.9 collective-permute-start.5
  251.6 1.1 fusion.1
  253.5 1.2 shard_map.105
  254.6 11.3 %all-to-all-done.10 = bf16[16,64,128]{2,1,0:T(8,128)(2,1)S(1)} async-done(((bf16[16,64,128]{2,1,0:T(8,128)(2,1)}), bf16[16,64,128]{2,1,0:T(8,128)(2,1)S(1)}, u32[]{:S(2)}, u32[]{:S(2)}) %all-to-all-start.10) | async-done | bytes 262176 | tf_op jit(solution)/shard_map/all_to_all | solution.py:328
  (25 shorter events, 7.4 us)
Async XLA Ops:
  0.7 1.0 copy-start.2
  1.7 0.9 copy-start.3
  2.6 0.8 copy-start.4
  69.5 3.8 %collective-permute-start = (bf16[16,128,128]{2,1,0:T(8,128)(2,1)S(1)}, bf16[16,128,128]{2,1,0:T(8,128)(2,1)S(1)}, u32[]{:S(2)}, u32[]{:S(2)}) collective-permute-start(bf16[16,128,128]{2,1,0:T(8,128)(2,1)S(1)} %all_to_all.61.pown_ref), channel_id=1, source_target_pairs={{0,16},{16,0},{32,48},{48,32},{64,80},{80,64},{96,112},{112,96},{1... | collective-permute-start | bytes 1572872 | tf_op jit(solution)/shard_map/ppermute | solution.py:349
  74.6 4.6 %collective-permute-start.1 = (bf16[16,272,128]{2,1,0:T(8,128)(2,1)S(1)}, bf16[16,272,128]{2,1,0:T(8,128)(2,1)S(1)}, u32[]{:S(2)}, u32[]{:S(2)}) collective-permute-start(bf16[16,272,128]{2,1,0:T(8,128)(2,1)S(1)} %get-tuple-element.28), channel_id=1, source_target_pairs={{0,16},{16,0},{32,48},{48,32},{64,80},{80,64},{96,112},{112,96},{1... | collective-permute-start | bytes 3342344 | tf_op jit(solution)/shard_map/ppermute | solution.py:358
  101.1 29.0 %copy-start = (bf16[1,2048,128]{2,1,0:T(8,128)(2,1)S(1)}, bf16[1,2048,128]{2,1,0:T(8,128)(2,1)}, u32[]{:S(2)}) copy-start(bf16[1,2048,128]{2,1,0:T(8,128)(2,1)} %param.7) | copy-start | bytes 1572868
  101.1 29.0 %copy-start.1 = (bf16[1,128,2048]{2,1,0:T(8,128)(2,1)S(1)}, bf16[1,128,2048]{2,1,0:T(8,128)(2,1)}, u32[]{:S(2)}) copy-start(bf16[1,128,2048]{2,1,0:T(8,128)(2,1)} %param.8) | copy-start | bytes 1572868
  178.7 4.6 %collective-permute-start.2 = (bf16[16,272,128]{2,1,0:T(8,128)(2,1)S(1)}, bf16[16,272,128]{2,1,0:T(8,128)(2,1)S(1)}, u32[]{:S(2)}, u32[]{:S(2)}) collective-permute-start(bf16[16,272,128]{2,1,0:T(8,128)(2,1)S(1)} %all_to_all.67.own_ref), channel_id=1, source_target_pairs={{0,16},{16,0},{32,48},{48,32},{64,80},{80,64},{96,112},{112,96},{1... | collective-permute-start | bytes 3342344 | tf_op jit(solution)/shard_map/ppermute | solution.py:382
  184.8 3.9 %collective-permute-start.3 = (bf16[16,144,128]{2,1,0:T(8,128)(2,1)S(1)}, bf16[16,144,128]{2,1,0:T(8,128)(2,1)S(1)}, u32[]{:S(2)}, u32[]{:S(2)}) collective-permute-start(bf16[16,144,128]{2,1,0:T(8,128)(2,1)S(1)} %get-tuple-element.36), channel_id=1, source_target_pairs={{0,16},{16,0},{32,48},{48,32},{64,80},{80,64},{96,112},{112,96},{1... | collective-permute-start | bytes 1769480 | tf_op jit(solution)/shard_map/ppermute | solution.py:396
  231.4 11.6 %all-to-all-start.11 = ((bf16[16,8,128]{2,1,0:T(8,128)(2,1)}), bf16[16,8,128]{2,1,0:T(8,128)(2,1)S(1)}, u32[]{:S(2)}, u32[]{:S(2)}) async-start(bf16[16,8,128]{2,1,0:T(8,128)(2,1)} %get-tuple-element.44), calls=%async_computation.11 | async-start | bytes 65536 | tf_op jit(solution)/shard_map/all_to_all | solution.py:328
  235.3 3.1 %collective-permute-start.4 = (f32[8,128]{1,0:T(8,128)S(1)}, f32[8,128]{1,0:T(8,128)S(1)}, u32[]{:S(2)}, u32[]{:S(2)}) collective-permute-start(f32[8,128]{1,0:T(8,128)S(1)} %get-tuple-element.39.colown_ref), channel_id=1, source_target_pairs={{0,16},{16,0},{32,48},{48,32},{64,80},{80,64},{96,112},{112,96},{1... | collective-permute-start | bytes 12296 | tf_op jit(solution)/shard_map/ppermute | solution.py:409
  242.9 23.0 %all-to-all-start.10 = ((bf16[16,64,128]{2,1,0:T(8,128)(2,1)}), bf16[16,64,128]{2,1,0:T(8,128)(2,1)S(1)}, u32[]{:S(2)}, u32[]{:S(2)}) async-start(bf16[16,64,128]{2,1,0:T(8,128)(2,1)} %shard_map.104), calls=%async_computation.10 | async-start | bytes 524288 | tf_op jit(solution)/shard_map/all_to_all | solution.py:328
  249.7 3.8 %collective-permute-start.5 = (bf16[16,8,128]{2,1,0:T(8,128)(2,1)S(1)}, bf16[16,8,128]{2,1,0:T(8,128)(2,1)S(1)}, u32[]{:S(2)}, u32[]{:S(2)}) collective-permute-start(bf16[16,8,128]{2,1,0:T(8,128)(2,1)S(1)} %all-to-all-done.11.own_ref), channel_id=1, source_target_pairs={{0,16},{16,0},{32,48},{48,32},{64,80},{80,64},{96,112},{112,96},{1... | collective-permute-start | bytes 98312 | tf_op jit(solution)/shard_map/ppermute | solution.py:424

commit v4 on v3

--- a/solution.py
+++ b/solution.py
@@ -50,11 +50,6 @@
     return jnp.concatenate([ref[f, rows, :] for f in range(16)], axis=1)
 
 
-def tokens_of(z_ref):
-    count = (z_ref.shape[1] - 8) // 2
-    return lanes(z_ref, slice(0, count)), lanes(z_ref, slice(count, 2 * count))
-
-
 def stage_kernel(at_ref, x_ref, g_ref, slot_ref, pay_ref):
     count = x_ref.shape[1]
     feats = pl.ds(pl.multiple_of(at_ref[1] * 128, 128), 128)
@@ -66,27 +61,47 @@
         pay_ref[e, 2 * count : 2 * count + 8, :] = piece
 
 
-def route_kernel(pown_ref, pother_ref, z_ref, own_ref, other_ref, logit_ref, comb_ref):
-    x, g = tokens_of(z_ref)
-    logits = jnp.concatenate([nt(x, lanes(ref)) for ref in (pown_ref, pother_ref)], axis=1)
+def route_kernel(p_ref, z_ref, sib_ref, logit_ref, stat_ref, x_ref, g_ref):
+    count = (z_ref.shape[1] - 8) // 2
+    for at, ref in enumerate((z_ref, sib_ref)):
+        rows = slice(at * count, (at + 1) * count)
+        x_ref[rows, :] = lanes(ref, slice(0, count))
+        g_ref[rows, :] = lanes(ref, slice(count, 2 * count))
+    logits = nt(x_ref[...], lanes(p_ref))
     logit_ref[...] = logits
+    peak = jnp.max(logits, axis=1, keepdims=True)
+    total = jnp.sum(jnp.exp(logits - peak), axis=1, keepdims=True)
+    lane = lax.broadcasted_iota(jnp.int32, logits.shape, 1)
+    stat_ref[...] = jnp.where(lane == 0, peak, total)
+
+
+def swapped(ref):
+    count = ref.shape[0] // 2
+    return jnp.concatenate([ref[count:, :], ref[:count, :]], axis=0)
+
+
+def share_kernel(logit_ref, stat_ref, sib_ref, x_ref, g_ref, pay_ref, comb_ref):
+    logits = logit_ref[...]
     peak = jnp.max(logits, axis=0, keepdims=True)
     raised = jnp.exp(logits - peak)
     total = jnp.sum(raised, axis=0, keepdims=True)
-    lifted = jnp.exp(logits - jnp.max(logits, axis=1, keepdims=True))
-    combine = lifted / jnp.sum(lifted, axis=1, keepdims=True)
+    mine, other = stat_ref[...], swapped(sib_ref)
+    top = jnp.maximum(mine[:, 0:1], other[:, 0:1])
+    over = mine[:, 1:2] * jnp.exp(mine[:, 0:1] - top) + other[:, 1:2] * jnp.exp(
+        other[:, 0:1] - top
+    )
+    combine = jnp.exp(logits - top) / over
     comb_ref[...] = combine
     stats = jnp.concatenate(
-        split3(peak) + split3(total) + [jnp.zeros((10, 256), F32)], axis=0
+        split3(peak) + split3(total) + [jnp.zeros((10, 128), F32)], axis=0
     ).astype(BF)
-    for pay_ref, cols in ((own_ref, slice(0, 128)), (other_ref, slice(128, 256))):
-        part_in = tn(raised[:, cols].astype(BF), x).astype(BF)
-        part_grad = tn(combine[:, cols].astype(BF), g).astype(BF)
-        for f in range(16):
-            feats = slice(f * 128, (f + 1) * 128)
-            pay_ref[f, 0:128, :] = part_in[:, feats]
-            pay_ref[f, 128:256, :] = part_grad[:, feats]
-            pay_ref[f, 256:272, :] = stats[:, cols]
+    part_in = tn(raised.astype(BF), x_ref[...]).astype(BF)
+    part_grad = tn(combine.astype(BF), g_ref[...]).astype(BF)
+    for f in range(16):
+        feats = slice(f * 128, (f + 1) * 128)
+        pay_ref[f, 0:128, :] = part_in[:, feats]
+        pay_ref[f, 128:256, :] = part_grad[:, feats]
+        pay_ref[f, 256:272, :] = stats
 
 
 def rescale(stats):
@@ -98,20 +113,6 @@
     rows = split3(peak) + split3(total)
     pad = jnp.zeros((122 - len(stats), 128), F32)
     return rows, jnp.concatenate([scale] + rows + [pad], axis=0).T
-
-
-def merge_core_kernel(own_ref, sib_ref, pay_ref):
-    rows, columns = rescale([ref[0, 256:272, :].astype(F32) for ref in (own_ref, sib_ref)])
-    stats = jnp.concatenate(rows + [jnp.zeros((10, 128), F32)], axis=0).astype(BF)
-    for f in range(16):
-        pay_ref[f, 0:128, :] = (
-            columns[:, 0:1] * own_ref[f, 0:128, :].astype(F32)
-            + columns[:, 1:2] * sib_ref[f, 0:128, :].astype(F32)
-        ).astype(BF)
-        pay_ref[f, 128:256, :] = (
-            own_ref[f, 128:256, :].astype(F32) + sib_ref[f, 128:256, :].astype(F32)
-        ).astype(BF)
-        pay_ref[f, 256:272, :] = stats
 
 
 def merge_seq_kernel(r_ref, pay_ref):
@@ -210,72 +211,64 @@
 
 
 def mix_kernel(
-    own_ref, other_ref, z_ref, logit_ref, comb_ref,
-    mixed_ref, parown_ref, parother_ref, guess_ref, disp_ref, cot_ref, term_ref, in_ref,
+    r_ref, x_ref, g_ref, logit_ref, comb_ref,
+    mixed_ref, other_ref, row_ref, guess_ref, col_ref, disp_ref, cot_ref, ccot_ref, in_ref,
 ):
-    x, g = tokens_of(z_ref)
-    combine = comb_ref[...]
-    combine_low = combine.astype(BF)
-    pair = (own_ref, other_ref)
-    stats = [ref[0, 256:272, :].astype(F32) for ref in pair]
-    logs = jnp.concatenate([s[0:1] + s[1:2] + s[2:3] for s in stats], axis=1)
-    sums = [
-        functools.reduce(jnp.add, [ref[f, 256:272, :].astype(F32) for f in range(16)])
-        for ref in pair
-    ]
-    guess = jnp.concatenate([s[3:4] + s[4:5] + s[5:6] for s in sums], axis=1)
-    outs = jnp.concatenate([lanes(ref, slice(0, 128)) for ref in pair], axis=0)
-    ins = jnp.concatenate([lanes(ref, slice(128, 256)) for ref in pair], axis=0)
-    dispatch_cot = nt(x, ins)
-    dispatch = jnp.exp(logit_ref[...] - logs)
+    count = mixed_ref.shape[0]
+    combine_low = comb_ref[...].astype(BF)
+    stats = [r_ref[f, 256:272, :].astype(F32) for f in range(16)]
+    guess = functools.reduce(jnp.add, stats)
+    guess = guess[3:4] + guess[4:5] + guess[5:6]
+    outs = lanes(r_ref, slice(0, 128))
+    ins = lanes(r_ref, slice(128, 256))
+    combine_cot = nt(g_ref[...], outs)
+    row = jnp.sum(combine_low.astype(F32) * combine_cot, axis=1, keepdims=True)
+    row_ref[...] = jnp.broadcast_to(row, combine_cot.shape)
+    dispatch_cot = nt(x_ref[...], ins)
+    dispatch = jnp.exp(logit_ref[...] - column_of(stats[0]))
     column = jnp.sum(dispatch.astype(BF).astype(F32) * dispatch_cot, axis=0, keepdims=True)
-    combine_cot = nt(g, outs)
-    row_sum = jnp.sum(combine_low.astype(F32) * combine_cot, axis=1, keepdims=True)
-    term = combine * (combine_cot - row_sum)
-    logit_low = (dispatch * (dispatch_cot - guess) + term).astype(BF)
-    for ref, half in ((parown_ref, slice(0, 128)), (parother_ref, slice(128, 256))):
-        part = tn(logit_low[:, half], x).astype(BF)
-        sums = jnp.concatenate(
-            split3(column[:, half]) + [jnp.zeros((13, 128), F32)], axis=0
-        ).astype(BF)
-        for f in range(16):
-            ref[f, 0:128, :] = part[:, f * 128 : (f + 1) * 128]
-            ref[f, 128:144, :] = sums
-    mixed = nn(combine_low, outs).astype(BF)
-    for f in range(16):
-        mixed_ref[f] = mixed[:, f * 128 : (f + 1) * 128]
-    guess_ref[...] = jnp.broadcast_to(guess, (8, 256))
+    mixed = nn(combine_low, outs)
+    mixed_ref[...] = mixed[:count]
+    other_ref[...] = mixed[count:]
+    guess_ref[...] = jnp.broadcast_to(guess, (8, 128))
+    col_ref[...] = jnp.broadcast_to(column, (8, 128))
     disp_ref[...] = dispatch
     cot_ref[...] = dispatch_cot
+    ccot_ref[...] = combine_cot
+    in_ref[...] = ins
+
+
+def logit_kernel(
+    row_ref, sib_ref, guess_ref, col_ref, disp_ref, cot_ref, ccot_ref, comb_ref, x_ref,
+    term_ref, pay_ref,
+):
+    row = row_ref[...] + swapped(sib_ref)
+    term = comb_ref[...] * (ccot_ref[...] - row)
     term_ref[...] = term
-    in_ref[...] = ins
+    logit_low = (disp_ref[...] * (cot_ref[...] - guess_ref[0:1, :]) + term).astype(BF)
+    part = tn(logit_low, x_ref[...]).astype(BF)
+    sums = jnp.concatenate(
+        split3(col_ref[0:1, :]) + [jnp.zeros((13, 128), F32)], axis=0
+    ).astype(BF)
+    for f in range(16):
+        pay_ref[f, 0:128, :] = part[:, f * 128 : (f + 1) * 128]
+        pay_ref[f, 128:144, :] = sums
 
 
 def column_of(block):
     return block[0:1] + block[1:2] + block[2:3]
 
 
-def param_core_kernel(own_ref, sib_ref, pay_ref):
-    sums = [ref[0, 128:144, :].astype(F32) for ref in (own_ref, sib_ref)]
-    sums = jnp.concatenate(
-        split3(column_of(sums[0]) + column_of(sums[1])) + [jnp.zeros((13, 128), F32)], axis=0
-    ).astype(BF)
-    for f in range(16):
-        pay_ref[f, 0:128, :] = (
-            own_ref[f, 0:128, :].astype(F32) + sib_ref[f, 0:128, :].astype(F32)
-        ).astype(BF)
-        pay_ref[f, 128:144, :] = sums
-
-
-def param_seq_kernel(r_ref, mixed_ref, pay_ref):
-    count = mixed_ref.shape[1]
+def param_seq_kernel(r_ref, mixed_ref, sib_ref, pay_ref):
+    count = mixed_ref.shape[0]
     total = functools.reduce(jnp.add, [r_ref[i, 0:128, :].astype(F32) for i in range(16)])
     column = functools.reduce(
         jnp.add, [column_of(r_ref[i, 128:144, :].astype(F32)) for i in range(16)]
     )
     sums = jnp.concatenate(split3(column) + [jnp.zeros((5, 128), F32)], axis=0)
     for e in range(16):
-        pay_ref[e, 0:count, :] = mixed_ref[e]
+        feats = slice(e * 128, (e + 1) * 128)
+        pay_ref[e, 0:count, :] = (mixed_ref[:, feats] + sib_ref[:, feats]).astype(BF)
         pay_ref[e, count : count + 16, :] = jnp.concatenate(
             [total[e * 8 : (e + 1) * 8], sums], axis=0
         ).astype(BF)
@@ -288,33 +281,38 @@
     )
     column = column_of(total[8:16])
     col_ref[...] = jnp.broadcast_to(column, (8, 128))
-    missed = column - guess_ref[0:1, 0:128]
+    missed = column - guess_ref[0:1, :]
     lane = lax.broadcasted_iota(jnp.int32, (8, 128), 1)
     row = lax.broadcasted_iota(jnp.int32, (8, 128), 0)
     missed = jnp.sum(
         jnp.where(lane == at_ref[0] * 8 + row, missed, 0.0), axis=1, keepdims=True
     )
-    param = (total[0:8] - missed * slot_ref[...]).astype(BF)
+    param = total[0:8] - missed * slot_ref[...]
     for i in range(16):
         pay_ref[i] = param
 
 
 def token_kernel(
-    colown_ref, colother_ref, pown_ref, pother_ref, disp_ref, cot_ref, term_ref, in_ref, tok_ref
+    col_ref, p_ref, disp_ref, cot_ref, term_ref, in_ref, own_ref, other_ref
 ):
-    column = jnp.concatenate([colown_ref[0:1, :], colother_ref[0:1, :]], axis=1)
-    params = jnp.concatenate([lanes(pown_ref), lanes(pother_ref)], axis=0)
+    count = own_ref.shape[0]
     dispatch = disp_ref[...]
-    logit_low = (dispatch * (cot_ref[...] - column) + term_ref[...]).astype(BF)
-    token_grad = (nn(dispatch.astype(BF), in_ref[...]) + nn(logit_low, params)).astype(BF)
+    logit_low = (dispatch * (cot_ref[...] - col_ref[0:1, :]) + term_ref[...]).astype(BF)
+    token_grad = nn(dispatch.astype(BF), in_ref[...]) + nn(logit_low, lanes(p_ref))
+    own_ref[...] = token_grad[:count]
+    other_ref[...] = token_grad[count:]
+
+
+def token_pair_kernel(own_ref, sib_ref, tok_ref):
     for f in range(16):
-        tok_ref[f] = token_grad[:, f * 128 : (f + 1) * 128]
+        feats = slice(f * 128, (f + 1) * 128)
+        tok_ref[f] = (own_ref[:, feats] + sib_ref[:, feats]).astype(BF)
 
 
 def param_out_kernel(at_ref, own_ref, other_ref, out_ref):
     first = at_ref[2] == 0
     for f in range(16):
-        own, other = own_ref[f].astype(F32), other_ref[f].astype(F32)
+        own, other = own_ref[f], other_ref[f]
         out_ref[:, f * 128 : (f + 1) * 128] = jnp.concatenate(
             [jnp.where(first, own, other), jnp.where(first, other, own)], axis=0
         ).astype(BF)
@@ -322,6 +320,10 @@
 
 CHIPS = [list(range(0, 32, 2)), list(range(1, 32, 2))]
 SIBLING = [(i, i ^ 1) for i in range(32)]
+
+
+def sibling(array):
+    return lax.ppermute(array, "seq", SIBLING)
 
 
 def swap(array, axis, groups=None):
@@ -346,17 +348,15 @@
     z = swap(block, "expert")
     mine = z[:, 2 * count :].reshape(128, 128)
     params = swap(jnp.broadcast_to(mine[None], (16, 128, 128)), "seq", CHIPS)
-    params_other = lax.ppermute(params, "seq", SIBLING)
+    z_sibling = sibling(z)
 
     half = shape((16, 272, 128), BF)
-    slots = shape((count, 256), F32)
+    slots = shape((2 * count, 128), F32)
+    wide = shape((2 * count, 2048), BF)
     small = shape((16, 24, 128), BF)
     row = shape((8, 128), F32)
-    own, other, logits, combine = call(
-        route_kernel, (half, half, slots, slots), params, params_other, z
-    )
-    sibling = lax.ppermute(other, "seq", SIBLING)
-    pay = call(merge_core_kernel, half, own, sibling)
+    logits, stats, x, g = call(route_kernel, (slots, slots, wide, wide), params, z, z_sibling)
+    pay, combine = call(share_kernel, (half, slots), logits, stats, sibling(stats), x, g)
     pay = call(merge_seq_kernel, small, swap(pay, "seq", CHIPS))
     pay, slot_piece, log_piece = call(
         merge_expert_kernel, (shape((32, 16, 128), BF), row, row), swap(pay, "expert")
@@ -378,42 +378,45 @@
     w_in_grad = tn(slot_low, pre).astype(BF)
     pay = call(out_merge_kernel, small, swap(pay, "seq"), slot_piece, log_piece)
     pay = call(spread_kernel, half, swap(pay, "expert"))
-    own = swap(pay, "seq", CHIPS)
-    other = lax.ppermute(own, "seq", SIBLING)
-    part = shape((16, 144, 128), BF)
-    mixed, own, other, guess, dispatch, dispatch_cot, term, ins = call(
+    wide = shape((count, 2048), F32)
+    mixed, other, rows, guess, column, dispatch, dispatch_cot, combine_cot, ins = call(
         mix_kernel,
-        (
-            by_feature, part, part, shape((8, 256), F32),
-            slots, slots, slots, shape((256, 2048), BF),
-        ),
-        own,
-        other,
-        z,
+        (wide, wide, slots, row, row, slots, slots, slots, shape((128, 2048), BF)),
+        swap(pay, "seq", CHIPS),
+        x,
+        g,
         logits,
         combine,
     )
-    pay = call(param_core_kernel, part, own, lax.ppermute(other, "seq", SIBLING))
+    term, pay = call(
+        logit_kernel,
+        (slots, shape((16, 144, 128), BF)),
+        rows,
+        sibling(rows),
+        guess,
+        column,
+        dispatch,
+        dispatch_cot,
+        combine_cot,
+        combine,
+        x,
+    )
     pay = call(
-        param_seq_kernel, shape((16, count + 16, 128), BF), swap(pay, "seq", CHIPS), mixed
+        param_seq_kernel,
+        shape((16, count + 16, 128), BF),
+        swap(pay, "seq", CHIPS),
+        mixed,
+        sibling(other),
     )
     pay = swap(pay, "expert")
     mixed = pay[:, 0:count].reshape(tokens.shape)
     param_grad, column = call(
-        param_expert_kernel, (shape((16, 8, 128), BF), row), at, pay, guess, slot_piece
-    )
-    token_grad = call(
-        token_kernel,
-        by_feature,
-        column,
-        lax.ppermute(column, "seq", SIBLING),
-        params,
-        params_other,
-        dispatch,
-        dispatch_cot,
-        term,
-        ins,
-    )
+        param_expert_kernel, (shape((16, 8, 128), F32), row), at, pay, guess, slot_piece
+    )
+    own, other = call(
+        token_kernel, (wide, wide), column, params, dispatch, dispatch_cot, term, ins
+    )
+    token_grad = call(token_pair_kernel, by_feature, own, sibling(other))
     token_grad = swap(token_grad, "expert").reshape(tokens.shape)
     param_grad = swap(param_grad, "seq", CHIPS)
     param_grad = call(
@@ -421,7 +424,7 @@
         shape((16, 2048), BF),
         at,
         param_grad,
-        lax.ppermute(param_grad, "seq", SIBLING),
+        sibling(param_grad),
     )
     return (mixed, token_grad, param_grad, w_in_grad[None], w_out_grad[None])
 

time: 267 us -> 263 us (0.985)
  blocking collectives: 204 us -> 188 us
  waiting for transfers between devices: 24.8 us -> 31.6 us
  starting transfers between devices: 21.3 us -> 26.9 us
    all_to_all x10 -> x9, blocking collectives: 204 us -> 188 us  [swap(): lax.all_to_all(array, axis, split_axis=0, concat_axis=0, tiled=True, axis...]
    all_to_all x2 -> x3, waiting for transfers between devices: 14.6 us -> 27.2 us  [swap(): lax.all_to_all(array, axis, split_axis=0, concat_axis=0, tiled=True, axis...]
    ppermute x6, waiting for transfers between devices: 10.2 us -> 4.39 us  [sibling(): return lax.ppermute(array, 'seq', SIBLING)]
    all_to_all x2 -> x3, starting transfers between devices: 9.58 us -> 15.2 us  [swap(): lax.all_to_all(array, axis, split_axis=0, concat_axis=0, tiled=True, axis...]
    pallas_call x14 -> x15, Pallas kernels: 9.4 us -> 8.89 us  [call(): pl.pallas_call(body, out_shape=out_shape, in_specs=[smem if arg.dtype ==...]
  transfers between devices with their start and end apart: 8 -> 9, of which waited for: 7 -> 6; matrix products, arithmetic and copies ran while one was open for 1% -> 1% of each run, Pallas kernels for 1% -> 1%
where the time goes in v4:
time: 263 us; the launch traced here: 262 us
  blocking collectives  188 us (71%)
  waiting for transfers between devices  31.6 us (12%)
  starting transfers between devices  26.9 us (10%)
  Pallas kernels  8.89 us (3%)
  local copies, waits for them, and re-layouts  4.28 us (2%)
    all_to_all x9, blocking collectives, swap(): lax.all_to_all(array, axis, split_axis=0, concat_axis=0, tiled=True, axis...  188 us
    all_to_all x3, waiting for transfers between devices, swap(): lax.all_to_all(array, axis, split_axis=0, concat_axis=0, tiled=True, axis...  27.2 us
    all_to_all x3, starting transfers between devices, swap(): lax.all_to_all(array, axis, split_axis=0, concat_axis=0, tiled=True, axis...  15.2 us
    ppermute x6, starting transfers between devices, sibling(): return lax.ppermute(array, 'seq', SIBLING)  11.6 us
    pallas_call x15, Pallas kernels, call(): pl.pallas_call(body, out_shape=out_shape, in_specs=[smem if arg.dtype ==...  8.89 us
  transfers between devices with their start and end apart: 9, of which 6 were waited for; matrix products, arithmetic and copies ran while one was open for 1% of the time, Pallas kernels for 1%

profile of v4, /device:TPU:32, one launch (start us, length us, event | category | flops | bytes accessed | tf_op | source)
XLA Modules:
  0.0 262.2 jit_solution(1256488890469810054)
XLA Ops:
  0.7 0.9 copy-done.2
  1.7 0.9 copy-done.3
  2.6 0.8 copy-done.4
  4.1 48.1 %all_to_all.60.z_ref = bf16[16,136,128]{2,1,0:T(8,128)(2,1)S(1)} all-to-all(bf16[16,136,128]{2,1,0:T(8,128)(2,1)S(1)} %shard_map.92), channel_id=1, replica_groups=mesh['seq'=32,'expert'=16] {'expert'}, dimensions={0} | all-to-all | bytes 1114112 | tf_op jit(solution)/shard_map/all_to_all | solution.py:330
  52.1 1.9 collective-permute-start
  54.2 19.0 %all_to_all.61.p_ref = bf16[16,128,128]{2,1,0:T(8,128)(2,1)S(1)} all-to-all(bf16[16,128,128]{2,1,0:T(8,128)(2,1)S(1)} %broadcast_in_dim.14), channel_id=1, replica_groups={{0,32,64,96,128,160,192,224,256,288,320,352,384,416,448,480},{16,48,80,..., dimensions={0} | all-to-all | bytes 1048576 | tf_op jit(solution)/shard_map/all_to_all | solution.py:330
  73.6 1.9 collective-permute-start.1
  75.6 1.2 collective-permute-done.1.sib_ref
  77.3 21.5 %all_to_all.62.r_ref = bf16[16,272,128]{2,1,0:T(8,128)(2,1)S(1)} all-to-all(bf16[16,272,128]{2,1,0:T(8,128)(2,1)S(1)} %get-tuple-element.38), channel_id=1, replica_groups={{0,32,64,96,128,160,192,224,256,288,320,352,384,416,448,480},{16,48,80,..., dimensions={0} | all-to-all | bytes 2228224 | tf_op jit(solution)/shard_map/all_to_all | solution.py:330
  99.3 16.1 %all_to_all.63.r_ref = bf16[16,24,128]{2,1,0:T(8,128)(2,1)S(1)} all-to-all(bf16[16,24,128]{2,1,0:T(8,128)(2,1)S(1)} %shard_map.95), channel_id=1, replica_groups=mesh['seq'=32,'expert'=16] {'expert'}, dimensions={0} | all-to-all | bytes 196608 | tf_op jit(solution)/shard_map/all_to_all | solution.py:330
  115.7 11.5 %all_to_all.64.r_ref = bf16[32,16,128]{2,1,0:T(8,128)(2,1)S(1)} all-to-all(bf16[32,16,128]{2,1,0:T(8,128)(2,1)S(1)} %get-tuple-element.39), channel_id=1, replica_groups=mesh['seq'=32,'expert'=16] {'seq'}, dimensions={0} | all-to-all | bytes 262144 | tf_op jit(solution)/shard_map/all_to_all | solution.py:330
  127.9 11.3 %all_to_all.65.r_ref = bf16[32,16,128]{2,1,0:T(8,128)(2,1)S(1)} all-to-all(bf16[32,16,128]{2,1,0:T(8,128)(2,1)S(1)} %get-tuple-element.40), channel_id=1, replica_groups=mesh['seq'=32,'expert'=16] {'seq'}, dimensions={0} | all-to-all | bytes 262144 | tf_op jit(solution)/shard_map/all_to_all | solution.py:330
  139.4 17.2 %all_to_all.66.r_ref = bf16[16,24,128]{2,1,0:T(8,128)(2,1)S(1)} all-to-all(bf16[16,24,128]{2,1,0:T(8,128)(2,1)S(1)} %shard_map.98), channel_id=1, replica_groups=mesh['seq'=32,'expert'=16] {'expert'}, dimensions={0} | all-to-all | bytes 196608 | tf_op jit(solution)/shard_map/all_to_all | solution.py:330
  156.7 19.1 %all_to_all.67.r_ref = bf16[16,272,128]{2,1,0:T(8,128)(2,1)S(1)} all-to-all(bf16[16,272,128]{2,1,0:T(8,128)(2,1)S(1)} %shard_map.99), channel_id=1, replica_groups={{0,32,64,96,128,160,192,224,256,288,320,352,384,416,448,480},{16,48,80,..., dimensions={0} | all-to-all | bytes 2228224 | tf_op jit(solution)/shard_map/all_to_all | solution.py:330
  176.4 1.9 collective-permute-start.2
  178.3 1.2 collective-permute-done.2.sib_ref
  179.5 1.2 shard_map.101
  180.7 3.6 %all-to-all-start.8 = ((bf16[16,144,128]{2,1,0:T(8,128)(2,1)}), bf16[16,144,128]{2,1,0:T(8,128)(2,1)S(1)}, u32[]{:S(2)}, u32[]{:S(2)}) async-start(bf16[16,144,128]{2,1,0:T(8,128)(2,1)} %get-tuple-element.50), calls=%async_computation.8 | async-start | bytes 1179648 | tf_op jit(solution)/shard_map/all_to_all | solution.py:330
  184.3 2.1 collective-permute-start.3
  186.4 1.9 collective-permute-done.3.sib_ref
  188.3 8.7 %all-to-all-done.8.r_ref = bf16[16,144,128]{2,1,0:T(8,128)(2,1)S(1)} async-done(((bf16[16,144,128]{2,1,0:T(8,128)(2,1)}), bf16[16,144,128]{2,1,0:T(8,128)(2,1)S(1)}, u32[]{:S(2)}, u32[]{:S(2)}) %all-to-all-start.8) | async-done | bytes 589856 | tf_op jit(solution)/shard_map/all_to_all | solution.py:330
  197.2 23.8 %all_to_all.68.r_ref = bf16[16,80,128]{2,1,0:T(8,128)(2,1)S(1)} all-to-all(bf16[16,80,128]{2,1,0:T(8,128)(2,1)S(1)} %shard_map.102), channel_id=1, replica_groups=mesh['seq'=32,'expert'=16] {'expert'}, dimensions={0} | all-to-all | bytes 655360 | tf_op jit(solution)/shard_map/all_to_all | solution.py:330
  221.0 1.3 shard_map.103
  222.7 1.9 collective-permute-start.4
  224.6 4.6 %all-to-all-start.11 = ((f32[16,8,128]{2,1,0:T(8,128)}), f32[16,8,128]{2,1,0:T(8,128)S(1)}, u32[]{:S(2)}, u32[]{:S(2)}) async-start(f32[16,8,128]{2,1,0:T(8,128)} %get-tuple-element.58), calls=%async_computation.11 | async-start | bytes 131072 | tf_op jit(solution)/shard_map/all_to_all | solution.py:330
  230.0 6.9 %all-to-all-done.11.own_ref = f32[16,8,128]{2,1,0:T(8,128)S(1)} async-done(((f32[16,8,128]{2,1,0:T(8,128)}), f32[16,8,128]{2,1,0:T(8,128)S(1)}, u32[]{:S(2)}, u32[]{:S(2)}) %all-to-all-start.11) | async-done | bytes 65568 | tf_op jit(solution)/shard_map/all_to_all | solution.py:330
  236.9 7.1 %all-to-all-start.10 = ((bf16[16,64,128]{2,1,0:T(8,128)(2,1)}), bf16[16,64,128]{2,1,0:T(8,128)(2,1)S(1)}, u32[]{:S(2)}, u32[]{:S(2)}) async-start(bf16[16,64,128]{2,1,0:T(8,128)(2,1)} %shard_map.105), calls=%async_computation.10 | async-start | bytes 524288 | tf_op jit(solution)/shard_map/all_to_all | solution.py:330
  243.9 1.1 fusion
  245.1 1.9 collective-permute-start.5
  247.0 1.1 fusion.1
  248.8 1.2 shard_map.106
  250.0 11.5 %all-to-all-done.10 = bf16[16,64,128]{2,1,0:T(8,128)(2,1)S(1)} async-done(((bf16[16,64,128]{2,1,0:T(8,128)(2,1)}), bf16[16,64,128]{2,1,0:T(8,128)(2,1)S(1)}, u32[]{:S(2)}, u32[]{:S(2)}) %all-to-all-start.10) | async-done | bytes 262176 | tf_op jit(solution)/shard_map/all_to_all | solution.py:330
  (29 shorter events, 6.9 us)
Async XLA Ops:
  0.7 1.0 copy-start.2
  1.7 0.9 copy-start.3
  2.6 0.8 copy-start.4
  52.1 21.0 %collective-permute-start = (bf16[16,136,128]{2,1,0:T(8,128)(2,1)S(1)}, bf16[16,136,128]{2,1,0:T(8,128)(2,1)S(1)}, u32[]{:S(2)}, u32[]{:S(2)}) collective-permute-start(bf16[16,136,128]{2,1,0:T(8,128)(2,1)S(1)} %all_to_all.60.z_ref), channel_id=1, source_target_pairs={{0,16},{16,0},{32,48},{48,32},{64,80},{80,64},{96,112},{112,96},{1... | collective-permute-start | bytes 1671176 | tf_op jit(solution)/shard_map/ppermute | solution.py:326
  73.6 3.1 %collective-permute-start.1 = (f32[128,128]{1,0:T(8,128)S(1)}, f32[128,128]{1,0:T(8,128)S(1)}, u32[]{:S(2)}, u32[]{:S(2)}) collective-permute-start(f32[128,128]{1,0:T(8,128)S(1)} %get-tuple-element.35.stat_ref), channel_id=1, source_target_pairs={{0,16},{16,0},{32,48},{48,32},{64,80},{80,64},{96,112},{112,96},{1... | collective-permute-start | bytes 196616 | tf_op jit(solution)/shard_map/ppermute | solution.py:326
  98.8 28.4 %copy-start = (bf16[1,2048,128]{2,1,0:T(8,128)(2,1)S(1)}, bf16[1,2048,128]{2,1,0:T(8,128)(2,1)}, u32[]{:S(2)}) copy-start(bf16[1,2048,128]{2,1,0:T(8,128)(2,1)} %param.7) | copy-start | bytes 1572868
  98.8 28.4 %copy-start.1 = (bf16[1,128,2048]{2,1,0:T(8,128)(2,1)S(1)}, bf16[1,128,2048]{2,1,0:T(8,128)(2,1)}, u32[]{:S(2)}) copy-start(bf16[1,128,2048]{2,1,0:T(8,128)(2,1)} %param.8) | copy-start | bytes 1572868
  176.4 4.3 %copy-start.5 = (f32[64,2048]{1,0:T(8,128)}, f32[64,2048]{1,0:T(8,128)S(1)}, u32[]{:S(2)}) copy-start(f32[64,2048]{1,0:T(8,128)S(1)} %get-tuple-element.52) | copy-start | bytes 1572868
  176.4 3.1 %collective-permute-start.2 = (f32[128,128]{1,0:T(8,128)S(1)}, f32[128,128]{1,0:T(8,128)S(1)}, u32[]{:S(2)}, u32[]{:S(2)}) collective-permute-start(f32[128,128]{1,0:T(8,128)S(1)} %get-tuple-element.44.row_ref), channel_id=1, source_target_pairs={{0,16},{16,0},{32,48},{48,32},{64,80},{80,64},{96,112},{112,96},{1... | collective-permute-start | bytes 196616 | tf_op jit(solution)/shard_map/ppermute | solution.py:326
  180.7 16.3 %all-to-all-start.8 = ((bf16[16,144,128]{2,1,0:T(8,128)(2,1)}), bf16[16,144,128]{2,1,0:T(8,128)(2,1)S(1)}, u32[]{:S(2)}, u32[]{:S(2)}) async-start(bf16[16,144,128]{2,1,0:T(8,128)(2,1)} %get-tuple-element.50), calls=%async_computation.8 | async-start | bytes 1179648 | tf_op jit(solution)/shard_map/all_to_all | solution.py:330
  184.3 4.0 %collective-permute-start.3 = (f32[64,2048]{1,0:T(8,128)}, f32[64,2048]{1,0:T(8,128)S(1)}, u32[]{:S(2)}, u32[]{:S(2)}) collective-permute-start(f32[64,2048]{1,0:T(8,128)} %copy-done.5), channel_id=1, source_target_pairs={{0,16},{16,0},{32,48},{48,32},{64,80},{80,64},{96,112},{112,96},{1... | collective-permute-start | bytes 1572872 | tf_op jit(solution)/shard_map/ppermute | solution.py:326
  222.7 6.5 %collective-permute-start.4 = (f32[64,2048]{1,0:T(8,128)S(1)}, f32[64,2048]{1,0:T(8,128)S(1)}, u32[]{:S(2)}, u32[]{:S(2)}) collective-permute-start(f32[64,2048]{1,0:T(8,128)S(1)} %get-tuple-element.57), channel_id=1, source_target_pairs={{0,16},{16,0},{32,48},{48,32},{64,80},{80,64},{96,112},{112,96},{1... | collective-permute-start | bytes 1572872 | tf_op jit(solution)/shard_map/ppermute | solution.py:326
  224.6 12.2 %all-to-all-start.11 = ((f32[16,8,128]{2,1,0:T(8,128)}), f32[16,8,128]{2,1,0:T(8,128)S(1)}, u32[]{:S(2)}, u32[]{:S(2)}) async-start(f32[16,8,128]{2,1,0:T(8,128)} %get-tuple-element.58), calls=%async_computation.11 | async-start | bytes 131072 | tf_op jit(solution)/shard_map/all_to_all | solution.py:330
  236.9 24.7 %all-to-all-start.10 = ((bf16[16,64,128]{2,1,0:T(8,128)(2,1)}), bf16[16,64,128]{2,1,0:T(8,128)(2,1)S(1)}, u32[]{:S(2)}, u32[]{:S(2)}) async-start(bf16[16,64,128]{2,1,0:T(8,128)(2,1)} %shard_map.105), calls=%async_computation.10 | async-start | bytes 524288 | tf_op jit(solution)/shard_map/all_to_all | solution.py:330
  245.1 3.8 %collective-permute-start.5 = (f32[16,8,128]{2,1,0:T(8,128)S(1)}, f32[16,8,128]{2,1,0:T(8,128)S(1)}, u32[]{:S(2)}, u32[]{:S(2)}) collective-permute-start(f32[16,8,128]{2,1,0:T(8,128)S(1)} %all-to-all-done.11.own_ref), channel_id=1, source_target_pairs={{0,16},{16,0},{32,48},{48,32},{64,80},{80,64},{96,112},{112,96},{1... | collective-permute-start | bytes 196616 | tf_op jit(solution)/shard_map/ppermute | solution.py:326

commit v5 on v4

--- a/solution.py
+++ b/solution.py
@@ -50,19 +50,27 @@
     return jnp.concatenate([ref[f, rows, :] for f in range(16)], axis=1)
 
 
-def stage_kernel(at_ref, x_ref, g_ref, slot_ref, pay_ref):
+def stage_kernel(chip_ref, core_ref, x_ref, g_ref, slot_ref, pay_ref):
     count = x_ref.shape[1]
-    feats = pl.ds(pl.multiple_of(at_ref[1] * 128, 128), 128)
+    feats = pl.ds(pl.multiple_of(chip_ref[0] * 128, 128), 128)
     both = slot_ref[:, feats].astype(F32)
-    piece = jnp.where(at_ref[2] == 0, both[0:8], both[8:16]).astype(BF)
+    piece = jnp.where(core_ref[0] == 0, both[0:8], both[8:16]).astype(BF)
     for e in range(16):
         pay_ref[e, 0:count, :] = x_ref[e]
         pay_ref[e, count : 2 * count, :] = g_ref[e]
         pay_ref[e, 2 * count : 2 * count + 8, :] = piece
 
 
+def split_kernel(z_ref, tok_ref, par_ref):
+    count = tok_ref.shape[1]
+    piece = jnp.concatenate([z_ref[e].astype(F32)[count:] for e in range(16)], axis=0).astype(BF)
+    for i in range(16):
+        tok_ref[i] = z_ref[i, 0:count, :]
+        par_ref[i] = piece
+
+
 def route_kernel(p_ref, z_ref, sib_ref, logit_ref, stat_ref, x_ref, g_ref):
-    count = (z_ref.shape[1] - 8) // 2
+    count = z_ref.shape[1] // 2
     for at, ref in enumerate((z_ref, sib_ref)):
         rows = slice(at * count, (at + 1) * count)
         x_ref[rows, :] = lanes(ref, slice(0, count))
@@ -309,8 +317,8 @@
         tok_ref[f] = (own_ref[:, feats] + sib_ref[:, feats]).astype(BF)
 
 
-def param_out_kernel(at_ref, own_ref, other_ref, out_ref):
-    first = at_ref[2] == 0
+def param_out_kernel(core_ref, own_ref, other_ref, out_ref):
+    first = core_ref[0] == 0
     for f in range(16):
         own, other = own_ref[f], other_ref[f]
         out_ref[:, f * 128 : (f + 1) * 128] = jnp.concatenate(
@@ -335,19 +343,25 @@
 def local(tokens, slot_params, w_in, w_out, out_grad):
     count = tokens.shape[1] // 16
     seq_at = lax.axis_index("seq")
-    at = jnp.stack([lax.axis_index("expert"), seq_at // 2, seq_at % 2]).astype(jnp.int32)
+    expert, chip, core = (
+        value.astype(jnp.int32).reshape(1)
+        for value in (lax.axis_index("expert"), seq_at // 2, seq_at % 2)
+    )
     by_feature = shape((16, count, 128), BF)
     block = call(
         stage_kernel,
         shape((16, 2 * count + 8, 128), BF),
-        at,
+        chip,
+        core,
         tokens.reshape(by_feature.shape),
         out_grad.reshape(by_feature.shape),
         slot_params,
     )
     z = swap(block, "expert")
-    mine = z[:, 2 * count :].reshape(128, 128)
-    params = swap(jnp.broadcast_to(mine[None], (16, 128, 128)), "seq", CHIPS)
+    z, params = call(
+        split_kernel, (shape((16, 2 * count, 128), BF), shape((16, 128, 128), BF)), z
+    )
+    params = swap(params, "seq", CHIPS)
     z_sibling = sibling(z)
 
     half = shape((16, 272, 128), BF)
@@ -411,7 +425,7 @@
     pay = swap(pay, "expert")
     mixed = pay[:, 0:count].reshape(tokens.shape)
     param_grad, column = call(
-        param_expert_kernel, (shape((16, 8, 128), F32), row), at, pay, guess, slot_piece
+        param_expert_kernel, (shape((16, 8, 128), F32), row), expert, pay, guess, slot_piece
     )
     own, other = call(
         token_kernel, (wide, wide), column, params, dispatch, dispatch_cot, term, ins
@@ -422,7 +436,7 @@
     param_grad = call(
         param_out_kernel,
         shape((16, 2048), BF),
-        at,
+        core,
         param_grad,
         sibling(param_grad),
     )

time: 263 us -> 263 us (level)
  blocking collectives: 188 us -> 164 us
  waiting for transfers between devices: 31.6 us -> 50.4 us
  starting transfers between devices: 26.9 us -> 32.6 us
    all_to_all x9 -> x8, blocking collectives: 188 us -> 164 us  [swap(): lax.all_to_all(array, axis, split_axis=0, concat_axis=0, tiled=True, axis...]
    all_to_all x3 -> x4, waiting for transfers between devices: 27.2 us -> 46.2 us  [swap(): lax.all_to_all(array, axis, split_axis=0, concat_axis=0, tiled=True, axis...]
    all_to_all x3 -> x4, starting transfers between devices: 15.2 us -> 20.9 us  [swap(): lax.all_to_all(array, axis, split_axis=0, concat_axis=0, tiled=True, axis...]
    pallas_call x15 -> x16, Pallas kernels: 8.89 us -> 8.2 us  [call(): pl.pallas_call(body, out_shape=out_shape, in_specs=[smem if arg.dtype ==...]
  transfers between devices with their start and end apart: 9 -> 10, of which waited for: 6 -> 7; matrix products, arithmetic and copies ran while one was open for 1% -> 1% of each run, Pallas kernels for 1% -> 1%
where the time goes in v5:
time: 263 us; the launch traced here: 262 us
  blocking collectives  164 us (62%)
  waiting for transfers between devices  50.4 us (19%)
  starting transfers between devices  32.6 us (12%)
  Pallas kernels  8.2 us (3%)
  local copies, waits for them, and re-layouts  4.17 us (2%)
    all_to_all x8, blocking collectives, swap(): lax.all_to_all(array, axis, split_axis=0, concat_axis=0, tiled=True, axis...  164 us
    all_to_all x4, waiting for transfers between devices, swap(): lax.all_to_all(array, axis, split_axis=0, concat_axis=0, tiled=True, axis...  46.2 us
    all_to_all x4, starting transfers between devices, swap(): lax.all_to_all(array, axis, split_axis=0, concat_axis=0, tiled=True, axis...  20.9 us
    ppermute x6, starting transfers between devices, sibling(): return lax.ppermute(array, 'seq', SIBLING)  11.7 us
    pallas_call x16, Pallas kernels, call(): pl.pallas_call(body, out_shape=out_shape, in_specs=[smem if arg.dtype ==...  8.2 us
  transfers between devices with their start and end apart: 10, of which 7 were waited for; matrix products, arithmetic and copies ran while one was open for 1% of the time, Pallas kernels for 1%

profile of v5, /device:TPU:32, one launch (start us, length us, event | category | flops | bytes accessed | tf_op | source)
XLA Modules:
  0.0 262.1 jit_solution(11813369998758886985)
XLA Ops:
  0.7 0.9 copy-done.2
  1.6 0.9 copy-done.3
  2.6 0.8 copy-done.4
  3.4 48.1 %all_to_all.60.z_ref = bf16[16,136,128]{2,1,0:T(8,128)(2,1)S(1)} all-to-all(bf16[16,136,128]{2,1,0:T(8,128)(2,1)S(1)} %shard_map.92), channel_id=1, replica_groups=mesh['seq'=32,'expert'=16] {'expert'}, dimensions={0} | all-to-all | bytes 1114112 | tf_op jit(solution)/shard_map/all_to_all | solution.py:338
  51.6 1.9 collective-permute-start
  53.6 19.0 %all_to_all.61.p_ref = bf16[16,128,128]{2,1,0:T(8,128)(2,1)S(1)} all-to-all(bf16[16,128,128]{2,1,0:T(8,128)(2,1)S(1)} %get-tuple-element.36), channel_id=1, replica_groups={{0,32,64,96,128,160,192,224,256,288,320,352,384,416,448,480},{16,48,80,..., dimensions={0} | all-to-all | bytes 1048576 | tf_op jit(solution)/shard_map/all_to_all | solution.py:338
  73.1 1.9 collective-permute-start.1
  75.0 1.2 collective-permute-done.1.sib_ref
  76.8 21.4 %all_to_all.62.r_ref = bf16[16,272,128]{2,1,0:T(8,128)(2,1)S(1)} all-to-all(bf16[16,272,128]{2,1,0:T(8,128)(2,1)S(1)} %get-tuple-element.42), channel_id=1, replica_groups={{0,32,64,96,128,160,192,224,256,288,320,352,384,416,448,480},{16,48,80,..., dimensions={0} | all-to-all | bytes 2228224 | tf_op jit(solution)/shard_map/all_to_all | solution.py:338
  98.8 16.1 %all_to_all.63.r_ref = bf16[16,24,128]{2,1,0:T(8,128)(2,1)S(1)} all-to-all(bf16[16,24,128]{2,1,0:T(8,128)(2,1)S(1)} %shard_map.96), channel_id=1, replica_groups=mesh['seq'=32,'expert'=16] {'expert'}, dimensions={0} | all-to-all | bytes 196608 | tf_op jit(solution)/shard_map/all_to_all | solution.py:338
  115.2 11.5 %all_to_all.64.r_ref = bf16[32,16,128]{2,1,0:T(8,128)(2,1)S(1)} all-to-all(bf16[32,16,128]{2,1,0:T(8,128)(2,1)S(1)} %get-tuple-element.43), channel_id=1, replica_groups=mesh['seq'=32,'expert'=16] {'seq'}, dimensions={0} | all-to-all | bytes 262144 | tf_op jit(solution)/shard_map/all_to_all | solution.py:338
  127.4 11.3 %all_to_all.65.r_ref = bf16[32,16,128]{2,1,0:T(8,128)(2,1)S(1)} all-to-all(bf16[32,16,128]{2,1,0:T(8,128)(2,1)S(1)} %get-tuple-element.44), channel_id=1, replica_groups=mesh['seq'=32,'expert'=16] {'seq'}, dimensions={0} | all-to-all | bytes 262144 | tf_op jit(solution)/shard_map/all_to_all | solution.py:338
  138.8 17.2 %all_to_all.66.r_ref = bf16[16,24,128]{2,1,0:T(8,128)(2,1)S(1)} all-to-all(bf16[16,24,128]{2,1,0:T(8,128)(2,1)S(1)} %shard_map.99), channel_id=1, replica_groups=mesh['seq'=32,'expert'=16] {'expert'}, dimensions={0} | all-to-all | bytes 196608 | tf_op jit(solution)/shard_map/all_to_all | solution.py:338
  156.1 19.1 %all_to_all.67.r_ref = bf16[16,272,128]{2,1,0:T(8,128)(2,1)S(1)} all-to-all(bf16[16,272,128]{2,1,0:T(8,128)(2,1)S(1)} %shard_map.100), channel_id=1, replica_groups={{0,32,64,96,128,160,192,224,256,288,320,352,384,416,448,480},{16,48,80,..., dimensions={0} | all-to-all | bytes 2228224 | tf_op jit(solution)/shard_map/all_to_all | solution.py:338
  175.8 1.9 collective-permute-start.2
  177.8 1.2 collective-permute-done.2.sib_ref
  179.0 1.2 shard_map.102
  180.2 3.6 %all-to-all-start.8 = ((bf16[16,144,128]{2,1,0:T(8,128)(2,1)}), bf16[16,144,128]{2,1,0:T(8,128)(2,1)S(1)}, u32[]{:S(2)}, u32[]{:S(2)}) async-start(bf16[16,144,128]{2,1,0:T(8,128)(2,1)} %get-tuple-element.54), calls=%async_computation.8 | async-start | bytes 1179648 | tf_op jit(solution)/shard_map/all_to_all | solution.py:338
  183.8 2.1 collective-permute-start.3
  185.8 1.7 collective-permute-done.3.sib_ref
  187.6 9.0 %all-to-all-done.8.r_ref = bf16[16,144,128]{2,1,0:T(8,128)(2,1)S(1)} async-done(((bf16[16,144,128]{2,1,0:T(8,128)(2,1)}), bf16[16,144,128]{2,1,0:T(8,128)(2,1)S(1)}, u32[]{:S(2)}, u32[]{:S(2)}) %all-to-all-start.8) | async-done | bytes 589856 | tf_op jit(solution)/shard_map/all_to_all | solution.py:338
  196.5 0.8 shard_map.103
  197.4 5.7 %all-to-all-start.9 = ((bf16[16,80,128]{2,1,0:T(8,128)(2,1)}), bf16[16,80,128]{2,1,0:T(8,128)(2,1)S(1)}, u32[]{:S(2)}, u32[]{:S(2)}) async-start(bf16[16,80,128]{2,1,0:T(8,128)(2,1)} %shard_map.103), calls=%async_computation.9 | async-start | bytes 655360 | tf_op jit(solution)/shard_map/all_to_all | solution.py:338
  203.0 18.3 %all-to-all-done.9.r_ref = bf16[16,80,128]{2,1,0:T(8,128)(2,1)S(1)} async-done(((bf16[16,80,128]{2,1,0:T(8,128)(2,1)}), bf16[16,80,128]{2,1,0:T(8,128)(2,1)S(1)}, u32[]{:S(2)}, u32[]{:S(2)}) %all-to-all-start.9) | async-done | bytes 327712 | tf_op jit(solution)/shard_map/all_to_all | solution.py:338
  222.5 1.9 collective-permute-start.4
  224.4 4.6 %all-to-all-start.11 = ((f32[16,8,128]{2,1,0:T(8,128)}), f32[16,8,128]{2,1,0:T(8,128)S(1)}, u32[]{:S(2)}, u32[]{:S(2)}) async-start(f32[16,8,128]{2,1,0:T(8,128)} %get-tuple-element.62), calls=%async_computation.11 | async-start | bytes 131072 | tf_op jit(solution)/shard_map/all_to_all | solution.py:338
  229.8 6.9 %all-to-all-done.11.own_ref = f32[16,8,128]{2,1,0:T(8,128)S(1)} async-done(((f32[16,8,128]{2,1,0:T(8,128)}), f32[16,8,128]{2,1,0:T(8,128)S(1)}, u32[]{:S(2)}, u32[]{:S(2)}) %all-to-all-start.11) | async-done | bytes 65568 | tf_op jit(solution)/shard_map/all_to_all | solution.py:338
  236.7 7.1 %all-to-all-start.10 = ((bf16[16,64,128]{2,1,0:T(8,128)(2,1)}), bf16[16,64,128]{2,1,0:T(8,128)(2,1)S(1)}, u32[]{:S(2)}, u32[]{:S(2)}) async-start(bf16[16,64,128]{2,1,0:T(8,128)(2,1)} %shard_map.106), calls=%async_computation.10 | async-start | bytes 524288 | tf_op jit(solution)/shard_map/all_to_all | solution.py:338
  243.8 1.1 fusion
  244.9 1.9 collective-permute-start.5
  246.8 1.1 fusion.1
  249.3 12.1 %all-to-all-done.10 = bf16[16,64,128]{2,1,0:T(8,128)(2,1)S(1)} async-done(((bf16[16,64,128]{2,1,0:T(8,128)(2,1)}), bf16[16,64,128]{2,1,0:T(8,128)(2,1)S(1)}, u32[]{:S(2)}, u32[]{:S(2)}) %all-to-all-start.10) | async-done | bytes 262176 | tf_op jit(solution)/shard_map/all_to_all | solution.py:338
  (26 shorter events, 7.6 us)
Async XLA Ops:
  0.7 1.0 copy-start.2
  1.6 0.9 copy-start.3
  2.6 0.8 copy-start.4
  51.6 20.9 %collective-permute-start = (bf16[16,128,128]{2,1,0:T(8,128)(2,1)S(1)}, bf16[16,128,128]{2,1,0:T(8,128)(2,1)S(1)}, u32[]{:S(2)}, u32[]{:S(2)}) collective-permute-start(bf16[16,128,128]{2,1,0:T(8,128)(2,1)S(1)} %get-tuple-element.37.z_ref), channel_id=1, source_target_pairs={{0,16},{16,0},{32,48},{48,32},{64,80},{80,64},{96,112},{112,96},{1... | collective-permute-start | bytes 1572872 | tf_op jit(solution)/shard_map/ppermute | solution.py:334
  73.1 3.1 %collective-permute-start.1 = (f32[128,128]{1,0:T(8,128)S(1)}, f32[128,128]{1,0:T(8,128)S(1)}, u32[]{:S(2)}, u32[]{:S(2)}) collective-permute-start(f32[128,128]{1,0:T(8,128)S(1)} %get-tuple-element.39.stat_ref), channel_id=1, source_target_pairs={{0,16},{16,0},{32,48},{48,32},{64,80},{80,64},{96,112},{112,96},{1... | collective-permute-start | bytes 196616 | tf_op jit(solution)/shard_map/ppermute | solution.py:334
  98.2 28.4 %copy-start = (bf16[1,2048,128]{2,1,0:T(8,128)(2,1)S(1)}, bf16[1,2048,128]{2,1,0:T(8,128)(2,1)}, u32[]{:S(2)}) copy-start(bf16[1,2048,128]{2,1,0:T(8,128)(2,1)} %param.7) | copy-start | bytes 1572868
  98.2 28.4 %copy-start.1 = (bf16[1,128,2048]{2,1,0:T(8,128)(2,1)S(1)}, bf16[1,128,2048]{2,1,0:T(8,128)(2,1)}, u32[]{:S(2)}) copy-start(bf16[1,128,2048]{2,1,0:T(8,128)(2,1)} %param.8) | copy-start | bytes 1572868
  175.8 3.1 %collective-permute-start.2 = (f32[128,128]{1,0:T(8,128)S(1)}, f32[128,128]{1,0:T(8,128)S(1)}, u32[]{:S(2)}, u32[]{:S(2)}) collective-permute-start(f32[128,128]{1,0:T(8,128)S(1)} %get-tuple-element.48.row_ref), channel_id=1, source_target_pairs={{0,16},{16,0},{32,48},{48,32},{64,80},{80,64},{96,112},{112,96},{1... | collective-permute-start | bytes 196616 | tf_op jit(solution)/shard_map/ppermute | solution.py:334
  180.2 16.3 %all-to-all-start.8 = ((bf16[16,144,128]{2,1,0:T(8,128)(2,1)}), bf16[16,144,128]{2,1,0:T(8,128)(2,1)S(1)}, u32[]{:S(2)}, u32[]{:S(2)}) async-start(bf16[16,144,128]{2,1,0:T(8,128)(2,1)} %get-tuple-element.54), calls=%async_computation.8 | async-start | bytes 1179648 | tf_op jit(solution)/shard_map/all_to_all | solution.py:338
  183.8 3.8 %collective-permute-start.3 = (f32[64,2048]{1,0:T(8,128)S(1)}, f32[64,2048]{1,0:T(8,128)S(1)}, u32[]{:S(2)}, u32[]{:S(2)}) collective-permute-start(f32[64,2048]{1,0:T(8,128)S(1)} %get-tuple-element.56), channel_id=1, source_target_pairs={{0,16},{16,0},{32,48},{48,32},{64,80},{80,64},{96,112},{112,96},{1... | collective-permute-start | bytes 1572872 | tf_op jit(solution)/shard_map/ppermute | solution.py:334
  197.4 24.0 %all-to-all-start.9 = ((bf16[16,80,128]{2,1,0:T(8,128)(2,1)}), bf16[16,80,128]{2,1,0:T(8,128)(2,1)S(1)}, u32[]{:S(2)}, u32[]{:S(2)}) async-start(bf16[16,80,128]{2,1,0:T(8,128)(2,1)} %shard_map.103), calls=%async_computation.9 | async-start | bytes 655360 | tf_op jit(solution)/shard_map/all_to_all | solution.py:338
  222.5 6.5 %collective-permute-start.4 = (f32[64,2048]{1,0:T(8,128)S(1)}, f32[64,2048]{1,0:T(8,128)S(1)}, u32[]{:S(2)}, u32[]{:S(2)}) collective-permute-start(f32[64,2048]{1,0:T(8,128)S(1)} %get-tuple-element.61), channel_id=1, source_target_pairs={{0,16},{16,0},{32,48},{48,32},{64,80},{80,64},{96,112},{112,96},{1... | collective-permute-start | bytes 1572872 | tf_op jit(solution)/shard_map/ppermute | solution.py:334
  224.4 12.2 %all-to-all-start.11 = ((f32[16,8,128]{2,1,0:T(8,128)}), f32[16,8,128]{2,1,0:T(8,128)S(1)}, u32[]{:S(2)}, u32[]{:S(2)}) async-start(f32[16,8,128]{2,1,0:T(8,128)} %get-tuple-element.62), calls=%async_computation.11 | async-start | bytes 131072 | tf_op jit(solution)/shard_map/all_to_all | solution.py:338
  236.7 24.7 %all-to-all-start.10 = ((bf16[16,64,128]{2,1,0:T(8,128)(2,1)}), bf16[16,64,128]{2,1,0:T(8,128)(2,1)S(1)}, u32[]{:S(2)}, u32[]{:S(2)}) async-start(bf16[16,64,128]{2,1,0:T(8,128)(2,1)} %shard_map.106), calls=%async_computation.10 | async-start | bytes 524288 | tf_op jit(solution)/shard_map/all_to_all | solution.py:338
  244.9 3.8 %collective-permute-start.5 = (f32[16,8,128]{2,1,0:T(8,128)S(1)}, f32[16,8,128]{2,1,0:T(8,128)S(1)}, u32[]{:S(2)}, u32[]{:S(2)}) collective-permute-start(f32[16,8,128]{2,1,0:T(8,128)S(1)} %all-to-all-done.11.own_ref), channel_id=1, source_target_pairs={{0,16},{16,0},{32,48},{48,32},{64,80},{80,64},{96,112},{112,96},{1... | collective-permute-start | bytes 196616 | tf_op jit(solution)/shard_map/ppermute | solution.py:334
